TPU v7x, 256 devices: a whole 4x4x8 slice. The times are simulated.
256 devices in a mesh: dev: 256 (over x, z, y, core).
Axes of the slice: x: 4, y: 4, z: 8, core: 2. Of those that a mesh axis runs over, the one named last changes fastest.
Arguments:
- state: float32 [5, 64, 131072], P(None, None, 'dev'), as said below
- step_size: float32 [1], replicated, may hold values from 0.0003 to 0.0006
- levels: int32 [131072], P('dev'), may hold values from 6 to 7, as said below
- send_faces: int32 [2048, 128], P('dev'), may hold values from 0 to 3072, as said below
- partner: int32 [6, 131072], P(None, 'dev'), may hold values from 0 to 4096, as said below
- mortar_in: int32 [5, 10240], P(None, 'dev'), may hold values from 0 to 4096, as said below
- mortar_dir: int32 [10240], P('dev'), may hold values from 0 to 3, as said below
- return_faces: int32 [512, 32], P('dev'), may hold values from 0 to 200, as said below
- flux_source: int32 [6, 131072], P(None, 'dev'), may hold values from 0 to 264, as said below
Outputs:
- increment: float32 [5, 64, 131072], P(None, None, 'dev')
Inputs may be any that keep to these rules, and one draw needn't show every extreme that they name: At every node the entries are density, momenta and total energy of a state with density from 1 to 1.5, velocity components from -0.2 to 0.2 and pressure from 1 to 1.5. `levels`: every element has level 6 or 7. `send_faces`: row 8 d + p lists local face numbers of device d whose traces its peer p needs; 3072 marks an empty entry. Faces are either conforming (opposite faces of two elements of one level, each the other's partner) or hanging (one face and four faces of elements one level finer meet in exactly one mortar); partners lie within 4 devices along the curve, mortars join faces of one device or of two adjacent ones. Hanging faces have partner 6 * 512. `mortar_in`: unused mortar entries name 3072 in all five rows. `mortar_dir`: unused mortar entries have 0. `return_faces`: 200 marks an empty entry. `flux_source`: 200 exactly for conforming faces.
All inputs are finite; a program needn't handle non-finite values.
Results may differ from a plain program's by a relative error of at most 0.0003.
Values sent between devices are 32-bit elements; how exact they have to be, the bound alone decides.
A program may use at most 64 MiB of HBM per device.

v0:
```python
import jax
import jax.numpy as jnp
import numpy as np
from jax import lax
from jax.sharding import PartitionSpec as P

GAMMA = 1.4
HIGHEST = lax.Precision.HIGHEST
ROW_WIDTH = 128


def passed_along(block, axis, distance):
    devices = range(lax.axis_size(axis))
    route = [((i - distance) % len(devices), i) for i in devices]
    return lax.ppermute(block, axis, route)


def lobatto_tables():
    nodes = np.array([-1.0, -1.0 / np.sqrt(5.0), 1.0 / np.sqrt(5.0), 1.0])
    weights = np.array([1.0, 5.0, 5.0, 1.0]) / 6.0

    def basis(points):
        table = np.ones((len(points), 4))
        for column in range(4):
            for other in range(4):
                if other != column:
                    table[:, column] *= (points - nodes[other]) / (nodes[column] - nodes[other])
        return table

    derivative = np.zeros((4, 4))
    for row in range(4):
        for column in range(4):
            total = 0.0
            for other in range(4):
                if other != column:
                    term = 1.0 / (nodes[column] - nodes[other])
                    for third in range(4):
                        if third != column and third != other:
                            term *= (nodes[row] - nodes[third]) / (nodes[column] - nodes[third])
                    total += term
            derivative[row, column] = total
    lower = basis((nodes - 1.0) / 2.0)
    upper = basis((nodes + 1.0) / 2.0)
    back_lower = 0.5 * (lower.T * weights[None, :]) / weights[:, None]
    back_upper = 0.5 * (upper.T * weights[None, :]) / weights[:, None]
    return [
        np.asarray(table, np.float32)
        for table in (derivative, lower, upper, back_lower, back_upper)
    ]


def face_normals(count):
    signs = np.zeros((3, 6), np.float32)
    for face in range(6):
        signs[face // 2, face] = 2.0 * (face % 2) - 1.0
    return tuple((jnp.asarray(np.repeat(signs[axis], count)) for axis in range(3)))


def reference_state(count):
    values = jnp.array([1.0, 0.0, 0.0, 0.0, 2.5], jnp.float32)
    return jnp.broadcast_to(values[:, None, None], (5, 16, count))


def normal_flux(state, normal):
    density = state[0]
    motion = [state[1 + axis] / density for axis in range(3)]
    pressure = (GAMMA - 1.0) * (
        state[4] - 0.5 * (state[1] * motion[0] + state[2] * motion[1] + state[3] * motion[2])
    )
    along = motion[0] * normal[0] + motion[1] * normal[1] + motion[2] * normal[2]
    flux = jnp.stack(
        [
            state[0] * along,
            state[1] * along + pressure * normal[0],
            state[2] * along + pressure * normal[1],
            state[3] * along + pressure * normal[2],
            (state[4] + pressure) * along,
        ]
    )
    speed = jnp.abs(along) + jnp.sqrt(GAMMA * pressure / density)
    return (flux, speed)


def rusanov(inside, inside_flux, inside_speed, outside, normal):
    outside_flux, outside_speed = normal_flux(outside, normal)
    return 0.5 * (inside_flux + outside_flux) - 0.5 * jnp.maximum(inside_speed, outside_speed) * (
        outside - inside
    )


def face_traces(block):
    cube = block.reshape(5, 4, 4, 4, block.shape[-1])
    faces = [
        cube[:, 0],
        cube[:, 3],
        cube[:, :, 0],
        cube[:, :, 3],
        cube[:, :, :, 0],
        cube[:, :, :, 3],
    ]
    return jnp.concatenate([face.reshape(5, 16, block.shape[-1]) for face in faces], axis=2)


def volume_term(block, scale):
    cube = block.reshape(5, 4, 4, 4, block.shape[-1])
    derivative = jnp.asarray(lobatto_tables()[0])
    first, _ = normal_flux(cube, (1.0, 0.0, 0.0))
    second, _ = normal_flux(cube, (0.0, 1.0, 0.0))
    third, _ = normal_flux(cube, (0.0, 0.0, 1.0))
    total = jnp.einsum("ai,vijke->vajke", derivative, first, precision=HIGHEST)
    total = total + jnp.einsum("bj,vijke->vibke", derivative, second, precision=HIGHEST)
    total = total + jnp.einsum("ck,vijke->vijce", derivative, third, precision=HIGHEST)
    return -scale * total


def add_lift(residual, jump, scale):
    count = residual.shape[-1]
    parts = -6.0 * scale * jump.reshape(5, 4, 4, 6, count)
    residual = residual.at[:, 0].add(parts[:, :, :, 0])
    residual = residual.at[:, 3].add(parts[:, :, :, 1])
    residual = residual.at[:, :, 0].add(parts[:, :, :, 2])
    residual = residual.at[:, :, 3].add(parts[:, :, :, 3])
    residual = residual.at[:, :, :, 0].add(parts[:, :, :, 4])
    residual = residual.at[:, :, :, 3].add(parts[:, :, :, 5])
    return residual


def mortar_fluxes(big, smalls, direction):
    tables = lobatto_tables()
    forward = (jnp.asarray(tables[1]), jnp.asarray(tables[2]))
    backward = (jnp.asarray(tables[3]), jnp.asarray(tables[4]))
    count = big.shape[-1]
    normal = tuple(
        (
            (direction == 2 * axis + 1).astype(jnp.float32)
            - (direction == 2 * axis).astype(jnp.float32)
            for axis in range(3)
        )
    )
    square = big.reshape(5, 4, 4, count)
    gathered = jnp.zeros_like(big)
    pieces = []
    for quarter in range(4):
        near = jnp.einsum(
            "ai,bj,vijm->vabm",
            forward[quarter % 2],
            forward[quarter // 2],
            square,
            precision=HIGHEST,
        ).reshape(5, 16, count)
        near_flux, near_speed = normal_flux(near, normal)
        star = rusanov(near, near_flux, near_speed, smalls[quarter], normal)
        pieces.append(-star)
        gathered = gathered + jnp.einsum(
            "ai,bj,vijm->vabm",
            backward[quarter % 2],
            backward[quarter // 2],
            star.reshape(5, 4, 4, count),
            precision=HIGHEST,
        ).reshape(5, 16, count)
    return jnp.concatenate([gathered] + pieces, axis=2)


def to_rows(columns):
    count = columns.shape[-1]
    flat = columns.reshape(80, count)
    return jnp.concatenate([flat, jnp.zeros((ROW_WIDTH - 80, count), jnp.float32)], axis=0).T


def from_rows(rows):
    return rows.T[:80].reshape(5, 16, rows.shape[0])


def body(
    state, step_size, levels, send_faces, partner, mortar_in, mortar_dir, return_faces, flux_source
):
    elems = state.shape[2]
    hop = send_faces.shape[0] // 2
    slots = send_faces.shape[1]
    mortar_count = mortar_dir.shape[0]
    return_count = return_faces.shape[1]
    empty_flux = 5 * mortar_count
    scale = jnp.exp2(levels.astype(jnp.float32) + 1.0)
    local = face_traces(state)
    padded = to_rows(jnp.concatenate([local, reference_state(1)], axis=2))
    outgoing = jnp.take(padded, send_faces.reshape(-1), axis=0).reshape(2 * hop, slots, ROW_WIDTH)
    arrived = []
    for peer in range(2 * hop):
        distance = peer + 1 if peer < hop else hop - 1 - peer
        arrived.append(passed_along(outgoing[peer], "dev", distance))
    incoming = jnp.concatenate(arrived, axis=0)
    table = jnp.concatenate([padded, incoming], axis=0)
    gathered = from_rows(jnp.take(table, mortar_in.reshape(-1), axis=0)).reshape(
        5, 16, 5, mortar_count
    )
    results = mortar_fluxes(
        gathered[:, :, 0], [gathered[:, :, 1 + quarter] for quarter in range(4)], mortar_dir
    )
    result_rows = jnp.concatenate(
        [to_rows(results), jnp.zeros((1, ROW_WIDTH), jnp.float32)], axis=0
    )
    leaving = jnp.take(result_rows, return_faces.reshape(-1), axis=0).reshape(
        2, return_count, ROW_WIDTH
    )
    returned = []
    for side in range(2):
        returned.append(passed_along(leaving[side], "dev", 1 - 2 * side))
    normals = face_normals(elems)
    local_flux, local_speed = normal_flux(local, normals)
    outside = from_rows(jnp.take(table, partner.reshape(-1), axis=0))
    conforming = rusanov(local, local_flux, local_speed, outside, normals)
    flux_table = jnp.concatenate([result_rows] + returned, axis=0)
    anchors = flux_source.reshape(-1)
    from_mortar = from_rows(jnp.take(flux_table, anchors, axis=0))
    star = jnp.where((anchors != empty_flux)[None, None, :], from_mortar, conforming)
    residual = add_lift(volume_term(state, scale), star - local_flux, scale)
    return step_size[0] * residual.reshape(5, 64, elems)


def solution(mesh):
    placed = (
        P(None, None, "dev"),
        P(),
        P("dev"),
        P("dev", None),
        P(None, "dev"),
        P(None, "dev"),
        P("dev"),
        P("dev", None),
        P(None, "dev"),
    )
    return jax.shard_map(
        body, mesh=mesh, in_specs=placed, out_specs=P(None, None, "dev"), check_vma=False
    )
```

profile of v0, /device:TPU:0, one launch (start us, length us, event | category | flops | bytes accessed | tf_op | source)
XLA Modules:
  0.0 188.1 jit_solution(17181824945316276602)
XLA Ops:
  8.0 2.8 %gather_fusion = f32[1024,128]{1,0:T(8,128)S(1)} fusion(f32[3073,128]{1,0:T(8,128)S(1)} %pad_bitcast_fusion, s32[1024]{0:T(1024)S(1)} %get-tuple-element.325), kind=kCustom, calls=%fused_computation | custom fusion | bytes 1052672 | tf_op jit(solution)/shard_map/jit(_take)/gather | solution.py:186
  12.0 2.1 %collective-permute-start.2 = (f32[128,128]{1,0:T(8,128)}, f32[128,128]{1,0:T(8,128)}, u32[]{:S(2)}, u32[]{:S(2)}) collective-permute-start(f32[128,128]{1,0:T(8,128)} %get-tuple-element.180), channel_id=1, source_target_pairs={{253,0},{254,1},{255,2},{0,3},{1,4},{2,5},{3,6},{4,7},{5,8},{6,9},... | collective-permute-start | bytes 196616 | tf_op jit(solution)/shard_map/ppermute | solution.py:15
  14.0 3.2 %collective-permute-start.3 = (f32[128,128]{1,0:T(8,128)}, f32[128,128]{1,0:T(8,128)}, u32[]{:S(2)}, u32[]{:S(2)}) collective-permute-start(f32[128,128]{1,0:T(8,128)} %get-tuple-element.179), channel_id=1, source_target_pairs={{252,0},{253,1},{254,2},{255,3},{0,4},{1,5},{2,6},{3,7},{4,8},{5,9... | collective-permute-start | bytes 196616 | tf_op jit(solution)/shard_map/ppermute | solution.py:15
  17.2 4.8 %collective-permute-start.4 = (f32[128,128]{1,0:T(8,128)}, f32[128,128]{1,0:T(8,128)}, u32[]{:S(2)}, u32[]{:S(2)}) collective-permute-start(f32[128,128]{1,0:T(8,128)} %get-tuple-element.178), channel_id=1, source_target_pairs={{1,0},{2,1},{3,2},{4,3},{5,4},{6,5},{7,6},{8,7},{9,8},{10,9},{11,1... | collective-permute-start | bytes 196616 | tf_op jit(solution)/shard_map/ppermute | solution.py:15
  35.6 1.3 fusion.7
  36.9 1.6 fusion.9
  40.2 1.9 %fusion.2 = f32[5,4,4,4,512]{4,1,3,2,0:T(4,128)S(1)} fusion(f32[5,4,4,4,512]{4,1,3,2,0:T(4,128)S(1)} %get-tuple-element.213, f32[4,4,1,1,1]{1,0,4,3,2:T(4,128)S(1)} %copy-done.88, f32[5,4,4,512,4]{3,4,2,1,0:T(4,128)S(1)} %fusion.7, f32[5,4,4,512,4]{3,4,2,1,0:T(4,128)S(1)} %fusion.9, f32[512]{0:T(512)S(1)} %get-tuple-element.249), kind=kOutput, calls=%fused_computation.11 | convolution fusion | flops 8355840 | bytes 2623552 | tf_op jit(solution)/shard_map/ai,vijke->vajke/dot_general | solution.py:110
  42.7 1.6 concatenate.78
  47.3 5.0 %collective-permute-start.7 = (f32[128,128]{1,0:T(8,128)S(1)}, f32[128,128]{1,0:T(8,128)S(1)}, u32[]{:S(2)}, u32[]{:S(2)}) collective-permute-start(f32[128,128]{1,0:T(8,128)S(1)} %copy-done.58), channel_id=1, source_target_pairs={{4,0},{5,1},{6,2},{7,3},{8,4},{9,5},{10,6},{11,7},{12,8},{13,9},{1... | collective-permute-start | bytes 196616 | tf_op jit(solution)/shard_map/ppermute | solution.py:15
  52.4 1.9 collective-permute-done.7
  54.2 8.3 %concatenate.72 = f32[4097,128]{1,0:T(8,128)S(1)} concatenate(f32[3073,128]{1,0:T(8,128)} %copy-done, f32[128,128]{1,0:T(8,128)S(1)} %collective-permute-done, f32[128,128]{1,0:T(8,128)} %collective-permute-done.1, f32[128,128]{1,0:T(8,128)} %collective-permute-done.2, f32[128,128]{1,0:T(8,128)} %collective-permute-done.3, f32[128,128]{1,0:T(8,128)} %collective-permute-done.4, ...), dimensions={0} | concatenate | bytes 4195328 | tf_op jit(solution)/shard_map/concatenate | solution.py:192
  70.5 11.9 %gather_fusion.4 = f32[3072,128]{1,0:T(8,128)} fusion(f32[4097,128]{1,0:T(8,128)S(1)} %concatenate.72, s32[3072]{0:T(1024)} %broadcast_clamp_fusion), kind=kCustom, calls=%fused_computation.4 | custom fusion | bytes 3158016 | tf_op jit(solution)/shard_map/jit(_take)/gather | solution.py:210
  82.4 3.1 %copy.442 = f32[3072,128]{0,1:T(8,128)} copy(f32[3072,128]{1,0:T(8,128)} %gather_fusion.4) | data formatting | bytes 3145728 | tf_op jit(solution)/shard_map/jit(_take)/gather | solution.py:210
  85.5 1.6 select_bitcast_fusion
  108.2 1.3 constant_dynamic-update-slice_fusion.81
  117.9 1.3 constant_dynamic-update-slice_fusion.61
  120.7 1.4 constant_dynamic-update-slice_fusion.57
  122.0 1.3 constant_dynamic-update-slice_fusion.56
  123.3 1.4 constant_dynamic-update-slice_fusion.52
  125.3 1.3 constant_dynamic-update-slice_fusion.46
  126.6 1.3 constant_dynamic-update-slice_fusion.41
  127.9 1.3 constant_dynamic-update-slice_fusion.36
  129.2 1.3 constant_dynamic-update-slice_fusion.31
  135.4 1.3 constant_dynamic-update-slice_fusion.26
  136.7 1.3 constant_dynamic-update-slice_fusion.21
  149.7 7.2 %collective-permute-start.9 = (f32[32,128]{1,0:T(8,128)S(1)}, f32[32,128]{1,0:T(8,128)S(1)}, u32[]{:S(2)}, u32[]{:S(2)}) collective-permute-start(f32[32,128]{1,0:T(8,128)S(1)} %get-tuple-element.247), channel_id=1, source_target_pairs={{1,0},{2,1},{3,2},{4,3},{5,4},{6,5},{7,6},{8,7},{9,8},{10,9},{11,1... | collective-permute-start | bytes 49160 | tf_op jit(solution)/shard_map/ppermute | solution.py:15
  161.2 1.7 reshape.9193
  163.0 8.1 %gather_fusion.3 = f32[3072,128]{1,0:T(8,128)S(1)} fusion(f32[265,128]{1,0:T(8,128)S(1)} %pad_maximum_fusion, s32[3072]{0:T(1024)S(1)} %copy-done.84), kind=kCustom, calls=%fused_computation.3 | custom fusion | bytes 3158016 | tf_op jit(solution)/shard_map/jit(_take)/gather | solution.py:214
  173.1 2.9 %reshape.9190 = f32[5,4,4,6,512]{4,3,2,1,0:T(8,128)} reshape(f32[80,3072]{1,0:T(8,128)} %slice.810) | data formatting | bytes 1966080 | tf_op jit(solution)/shard_map/reshape | solution.py:171
  176.0 4.9 %fusion.4 = f32[5,4,4,6,512]{4,1,3,2,0:T(4,128)S(1)} fusion(f32[5,4,4,6,512]{4,1,3,2,0:T(4,128)} %copy-done.17, f32[5,4,4,6,512]{4,3,2,1,0:T(8,128)} %reshape.9190, f32[5,4,4,6,512]{4,3,2,1,0:T(8,128)S(1)} %copy-done.3, f32[5,4,4,6,512]{4,3,2,1,0:T(8,128)S(1)} %copy-done.4, f32[5,4,4,6,512]{4,1,3,2,0:T(4,128)} %constant_dynamic-update-slice_fusion.117, ...), kind=kLoop, calls=%fused_computation.17 | loop fusion | flops 1966080 | bytes 6099968 | tf_op jit(solution)/shard_map/mul | solution.py:118
  182.1 1.5 scatter-add.20
  184.9 1.5 scatter-add.21
  (442 shorter events, 92.4 us)
Async XLA Ops:
  10.8 11.2 %copy-start.11 = (f32[5,1,4,4,512]{4,3,2,0,1:T(4,128)S(1)}, f32[5,1,4,4,512]{4,3,2,0,1:T(4,128)}, u32[]{:S(2)}) copy-start(f32[5,1,4,4,512]{4,3,2,0,1:T(4,128)} %copy-done.10) | copy-start | bytes 491524
  10.8 11.4 %copy-start.9 = (f32[5,4,1,4,512]{4,3,1,0,2:T(4,128)S(1)}, f32[5,4,1,4,512]{4,3,1,0,2:T(4,128)}, u32[]{:S(2)}) copy-start(f32[5,4,1,4,512]{4,3,1,0,2:T(4,128)} %copy-done.8) | copy-start | bytes 491524
  10.8 11.5 %copy-start.13 = (f32[5,4,4,1,512]{4,2,1,0,3:T(4,128)S(1)}, f32[5,4,4,1,512]{4,2,1,0,3:T(4,128)}, u32[]{:S(2)}) copy-start(f32[5,4,4,1,512]{4,2,1,0,3:T(4,128)} %copy-done.12) | copy-start | bytes 491524
  11.0 11.4 %copy-start.15 = (f32[5,4,4,1,512]{4,2,1,0,3:T(4,128)S(1)}, f32[5,4,4,1,512]{4,2,1,0,3:T(4,128)}, u32[]{:S(2)}) copy-start(f32[5,4,4,1,512]{4,2,1,0,3:T(4,128)} %copy-done.14) | copy-start | bytes 491524
  11.0 11.4 %copy-start.90 = (s32[5,40]{1,0:T(8,128)S(1)}, s32[5,40]{1,0:T(8,128)}, u32[]{:S(2)}) copy-start(s32[5,40]{1,0:T(8,128)} %param.35) | copy-start | bytes 2404
  11.0 12.2 %copy-start.36 = (s32[6,512]{1,0:T(8,128)S(1)}, s32[6,512]{1,0:T(8,128)}, u32[]{:S(2)}) copy-start(s32[6,512]{1,0:T(8,128)} %param.38) | copy-start | bytes 36868
  11.1 12.8 %copy-start.7 = (f32[5,64,512]{2,1,0:T(8,128)S(1)}, f32[5,64,512]{2,1,0:T(8,128)}, u32[]{:S(2)}) copy-start(f32[5,64,512]{2,1,0:T(8,128)} %param.30) | copy-start | bytes 1966084
  11.9 33.6 %collective-permute-start = (f32[128,128]{1,0:T(8,128)}, f32[128,128]{1,0:T(8,128)S(1)}, u32[]{:S(2)}, u32[]{:S(2)}) collective-permute-start(f32[128,128]{1,0:T(8,128)} %get-tuple-element.182), channel_id=1, source_target_pairs={{255,0},{0,1},{1,2},{2,3},{3,4},{4,5},{5,6},{6,7},{7,8},{8,9},{9,1... | collective-permute-start | bytes 196616 | tf_op jit(solution)/shard_map/ppermute | solution.py:15
  11.9 34.3 %collective-permute-start.1 = (f32[128,128]{1,0:T(8,128)}, f32[128,128]{1,0:T(8,128)}, u32[]{:S(2)}, u32[]{:S(2)}) collective-permute-start(f32[128,128]{1,0:T(8,128)} %get-tuple-element.181), channel_id=1, source_target_pairs={{254,0},{255,1},{0,2},{1,3},{2,4},{3,5},{4,6},{5,7},{6,8},{7,9},{8... | collective-permute-start | bytes 196616 | tf_op jit(solution)/shard_map/ppermute | solution.py:15
  12.0 35.3 %collective-permute-start.2 = (f32[128,128]{1,0:T(8,128)}, f32[128,128]{1,0:T(8,128)}, u32[]{:S(2)}, u32[]{:S(2)}) collective-permute-start(f32[128,128]{1,0:T(8,128)} %get-tuple-element.180), channel_id=1, source_target_pairs={{253,0},{254,1},{255,2},{0,3},{1,4},{2,5},{3,6},{4,7},{5,8},{6,9},... | collective-permute-start | bytes 196616 | tf_op jit(solution)/shard_map/ppermute | solution.py:15
  14.0 38.3 %collective-permute-start.3 = (f32[128,128]{1,0:T(8,128)}, f32[128,128]{1,0:T(8,128)}, u32[]{:S(2)}, u32[]{:S(2)}) collective-permute-start(f32[128,128]{1,0:T(8,128)} %get-tuple-element.179), channel_id=1, source_target_pairs={{252,0},{253,1},{254,2},{255,3},{0,4},{1,5},{2,6},{3,7},{4,8},{5,9... | collective-permute-start | bytes 196616 | tf_op jit(solution)/shard_map/ppermute | solution.py:15
  17.2 35.1 %collective-permute-start.4 = (f32[128,128]{1,0:T(8,128)}, f32[128,128]{1,0:T(8,128)}, u32[]{:S(2)}, u32[]{:S(2)}) collective-permute-start(f32[128,128]{1,0:T(8,128)} %get-tuple-element.178), channel_id=1, source_target_pairs={{1,0},{2,1},{3,2},{4,3},{5,4},{6,5},{7,6},{8,7},{9,8},{10,9},{11,1... | collective-permute-start | bytes 196616 | tf_op jit(solution)/shard_map/ppermute | solution.py:15
  42.1 10.3 %copy-start.1 = (f32[5,4,4,4,512]{4,1,3,2,0:T(4,128)}, f32[5,4,4,4,512]{4,1,3,2,0:T(4,128)S(1)}, u32[]{:S(2)}) copy-start(f32[5,4,4,4,512]{4,1,3,2,0:T(4,128)S(1)} %fusion.2) | copy-start | bytes 1966084
  45.5 6.8 %collective-permute-start.5 = (f32[128,128]{1,0:T(8,128)S(1)}, f32[128,128]{1,0:T(8,128)S(1)}, u32[]{:S(2)}, u32[]{:S(2)}) collective-permute-start(f32[128,128]{1,0:T(8,128)S(1)} %copy-done.60), channel_id=1, source_target_pairs={{2,0},{3,1},{4,2},{5,3},{6,4},{7,5},{8,6},{9,7},{10,8},{11,9},{12,... | collective-permute-start | bytes 196616 | tf_op jit(solution)/shard_map/ppermute | solution.py:15
  46.2 6.1 %collective-permute-start.6 = (f32[128,128]{1,0:T(8,128)S(1)}, f32[128,128]{1,0:T(8,128)S(1)}, u32[]{:S(2)}, u32[]{:S(2)}) collective-permute-start(f32[128,128]{1,0:T(8,128)S(1)} %copy-done.59), channel_id=1, source_target_pairs={{3,0},{4,1},{5,2},{6,3},{7,4},{8,5},{9,6},{10,7},{11,8},{12,9},{13... | collective-permute-start | bytes 196616 | tf_op jit(solution)/shard_map/ppermute | solution.py:15
  47.3 6.9 %collective-permute-start.7 = (f32[128,128]{1,0:T(8,128)S(1)}, f32[128,128]{1,0:T(8,128)S(1)}, u32[]{:S(2)}, u32[]{:S(2)}) collective-permute-start(f32[128,128]{1,0:T(8,128)S(1)} %copy-done.58), channel_id=1, source_target_pairs={{4,0},{5,1},{6,2},{7,3},{8,4},{9,5},{10,6},{11,7},{12,8},{13,9},{1... | collective-permute-start | bytes 196616 | tf_op jit(solution)/shard_map/ppermute | solution.py:15
  52.3 10.9 %copy-start.98 = (pred[200]{0:T(512)(128)(4,1)S(1)}, pred[200]{0:T(512)(128)(4,1)}, u32[]{:S(2)}) copy-start(pred[200]{0:T(512)(128)(4,1)} %compare_and_fusion.4) | copy-start | bytes 604
  92.4 7.7 %copy-start.40 = (f32[1,4,4,40]{3,2,1,0:T(4,128)}, f32[1,4,4,40]{3,2,1,0:T(4,128)S(1)}, u32[]{:S(2)}) copy-start(f32[1,4,4,40]{3,2,1,0:T(4,128)S(1)} %get-tuple-element.117) | copy-start | bytes 7684
  94.9 9.2 %copy-start.38 = (f32[1,4,4,40]{3,2,1,0:T(4,128)}, f32[1,4,4,40]{3,2,1,0:T(4,128)S(1)}, u32[]{:S(2)}) copy-start(f32[1,4,4,40]{3,2,1,0:T(4,128)S(1)} %get-tuple-element.232) | copy-start | bytes 7684
  94.9 9.2 %copy-start.39 = (f32[1,4,4,40]{3,2,1,0:T(4,128)}, f32[1,4,4,40]{3,2,1,0:T(4,128)S(1)}, u32[]{:S(2)}) copy-start(f32[1,4,4,40]{3,2,1,0:T(4,128)S(1)} %get-tuple-element.233) | copy-start | bytes 7684
  94.9 9.9 %copy-start.43 = (f32[1,4,4,40]{3,2,1,0:T(4,128)}, f32[1,4,4,40]{3,2,1,0:T(4,128)S(1)}, u32[]{:S(2)}) copy-start(f32[1,4,4,40]{3,2,1,0:T(4,128)S(1)} %get-tuple-element.228) | copy-start | bytes 7684
  97.5 7.3 %copy-start.44 = (f32[1,4,4,40]{3,2,1,0:T(4,128)}, f32[1,4,4,40]{3,2,1,0:T(4,128)S(1)}, u32[]{:S(2)}) copy-start(f32[1,4,4,40]{3,2,1,0:T(4,128)S(1)} %get-tuple-element.238) | copy-start | bytes 7684
  97.5 7.3 %copy-start.45 = (f32[1,4,4,40]{3,2,1,0:T(4,128)}, f32[1,4,4,40]{3,2,1,0:T(4,128)S(1)}, u32[]{:S(2)}) copy-start(f32[1,4,4,40]{3,2,1,0:T(4,128)S(1)} %get-tuple-element.239) | copy-start | bytes 7684
  100.8 30.4 %copy-start.32 = (f32[5,16,1,40]{3,2,1,0:T(1,128)S(1)}, f32[5,16,1,40]{3,2,1,0:T(1,128)}, u32[]{:S(2)}) copy-start(f32[5,16,1,40]{3,2,1,0:T(1,128)} %get-tuple-element.206) | copy-start | bytes 38404
  102.7 30.9 %copy-start.34 = (f32[5,16,1,40]{3,2,1,0:T(1,128)S(1)}, f32[5,16,1,40]{3,2,1,0:T(1,128)}, u32[]{:S(2)}) copy-start(f32[5,16,1,40]{3,2,1,0:T(1,128)} %get-tuple-element.208) | copy-start | bytes 38404
  104.8 33.9 %copy-start.33 = (f32[5,16,1,40]{3,2,1,0:T(1,128)S(1)}, f32[5,16,1,40]{3,2,1,0:T(1,128)}, u32[]{:S(2)}) copy-start(f32[5,16,1,40]{3,2,1,0:T(1,128)} %get-tuple-element.209) | copy-start | bytes 38404
  104.9 18.5 %copy-start.41 = (f32[1,4,4,40]{3,2,1,0:T(4,128)S(1)}, f32[1,4,4,40]{3,2,1,0:T(4,128)}, u32[]{:S(2)}) copy-start(f32[1,4,4,40]{3,2,1,0:T(4,128)} %copy-done.40) | copy-start | bytes 7684
  106.9 34.2 %copy-start.35 = (f32[5,16,1,40]{3,2,1,0:T(1,128)S(1)}, f32[5,16,1,40]{3,2,1,0:T(1,128)}, u32[]{:S(2)}) copy-start(f32[5,16,1,40]{3,2,1,0:T(1,128)} %get-tuple-element.207) | copy-start | bytes 38404
  111.7 32.9 %copy-start.86 = (f32[4,4,1,1]{1,0,3,2:T(4,128)S(1)}, f32[4,4,1,1]{1,0,3,2:T(4,128)}, u32[]{:S(2)}) copy-start(f32[4,4,1,1]{1,0,3,2:T(4,128)} %constant.316) | copy-start | bytes 196
  134.5 15.1 %copy-start.97 = (pred[64]{0:T(512)(128)(4,1)S(1)}, pred[64]{0:T(512)(128)(4,1)}, u32[]{:S(2)}) copy-start(pred[64]{0:T(512)(128)(4,1)} %compare_and_fusion.3) | copy-start | bytes 196
  149.6 13.2 %collective-permute-start.8 = (f32[32,128]{1,0:T(8,128)S(1)}, f32[32,128]{1,0:T(8,128)S(1)}, u32[]{:S(2)}, u32[]{:S(2)}) collective-permute-start(f32[32,128]{1,0:T(8,128)S(1)} %get-tuple-element.246), channel_id=1, source_target_pairs={{255,0},{0,1},{1,2},{2,3},{3,4},{4,5},{5,6},{6,7},{7,8},{8,9},{9,1... | collective-permute-start | bytes 49160 | tf_op jit(solution)/shard_map/ppermute | solution.py:15
  149.7 13.1 %collective-permute-start.9 = (f32[32,128]{1,0:T(8,128)S(1)}, f32[32,128]{1,0:T(8,128)S(1)}, u32[]{:S(2)}, u32[]{:S(2)}) collective-permute-start(f32[32,128]{1,0:T(8,128)S(1)} %get-tuple-element.247), channel_id=1, source_target_pairs={{1,0},{2,1},{3,2},{4,3},{5,4},{6,5},{7,6},{8,7},{9,8},{10,9},{11,1... | collective-permute-start | bytes 49160 | tf_op jit(solution)/shard_map/ppermute | solution.py:15
  (82 other events, 225.1 us)
where the time goes:
time: 191 us; the launch traced here: 188 us
  local copies, waits for them, and re-layouts  82.6 us (43%)
  other arithmetic  61 us (32%)
  starting transfers between devices  24.1 us (13%)
  matrix products  15.9 us (8%)
  between operations  2.67 us (1%)
    ppermute x10, starting transfers between devices, passed_along(): return lax.ppermute(block, axis, route)  24.1 us
    another operation x17, other arithmetic, normal_flux(): jnp.stack([state[0] * along, state[1] * along + pressure * normal[0], sta...  15.6 us
    gather x2, local copies, waits for them, and re-layouts, body(): outside = from_rows(jnp.take(table, partner.reshape(-1), axis=0))  15 us
    unnamed x26, other arithmetic  14.8 us
    unnamed x234, local copies, waits for them, and re-layouts  11.3 us
    gather x2, local copies, waits for them, and re-layouts, body(): from_mortar = from_rows(jnp.take(flux_table, anchors, axis=0))  8.59 us
    concatenate x1, local copies, waits for them, and re-layouts, body(): table = jnp.concatenate([padded, incoming], axis=0)  8.3 us
    dot_general x8, matrix products, mortar_fluxes(): jnp.einsum('ai,bj,vijm->vabm', backward[quarter % 2], backward[quarter //...  5.72 us
  transfers between devices with their start and end apart: 10, of which 1 were waited for; matrix products, arithmetic and copies ran while one was open for 14% of the time, Pallas kernels for 0%

commit v1 on v0

v1 whole, which is shorter than its diff:
```python
import functools
import jax
import jax.numpy as jnp
import numpy as np
from jax import lax
from jax.experimental import pallas as pl
from jax.experimental.pallas import tpu as pltpu
from jax.sharding import PartitionSpec as P

GAMMA = 1.4
HIGHEST = lax.Precision.HIGHEST
MESH = pl.DeviceIdType.MESH
TILES = 4
SIDE = (0, 0, 1, 1, 2, 2)


def lobatto_tables():
    nodes = np.array([-1.0, -1.0 / np.sqrt(5.0), 1.0 / np.sqrt(5.0), 1.0])
    weights = np.array([1.0, 5.0, 5.0, 1.0]) / 6.0

    def basis(points):
        table = np.ones((len(points), 4))
        for column in range(4):
            for other in range(4):
                if other != column:
                    table[:, column] *= (points - nodes[other]) / (nodes[column] - nodes[other])
        return table

    derivative = np.zeros((4, 4))
    for row in range(4):
        for column in range(4):
            total = 0.0
            for other in range(4):
                if other != column:
                    term = 1.0 / (nodes[column] - nodes[other])
                    for third in range(4):
                        if third != column and third != other:
                            term *= (nodes[row] - nodes[third]) / (nodes[column] - nodes[third])
                    total += term
            derivative[row, column] = total
    lower = basis((nodes - 1.0) / 2.0)
    upper = basis((nodes + 1.0) / 2.0)
    back_lower = 0.5 * (lower.T * weights[None, :]) / weights[:, None]
    back_upper = 0.5 * (upper.T * weights[None, :]) / weights[:, None]
    return [
        np.asarray(table, np.float32)
        for table in (derivative, lower, upper, back_lower, back_upper)
    ]


def mortar_matrices():
    _, lower, upper, back_lower, back_upper = [t.astype(np.float64) for t in lobatto_tables()]
    ahead, back = (lower, upper), (back_lower, back_upper)
    five = np.eye(5)
    forth = [np.kron(five, np.kron(ahead[q % 2], ahead[q // 2])) for q in range(4)]
    home = [np.kron(five, np.kron(back[q % 2], back[q // 2])) for q in range(4)]
    return np.concatenate(forth + home, axis=0).astype(np.float32)


def lanes_of(tile, index):
    return jnp.take_along_axis(tile, index, axis=1, mode="promise_in_bounds")


def axis_flux(parts, axis, sign):
    density, energy = parts[0], parts[4]
    inverse = 1.0 / density
    along = sign * parts[1 + axis] * inverse
    kinetic = parts[1] * parts[1] + parts[2] * parts[2] + parts[3] * parts[3]
    pressure = (GAMMA - 1.0) * (energy - 0.5 * kinetic * inverse)
    flux = [density * along]
    for other in range(3):
        term = parts[1 + other] * along
        flux.append(term + sign * pressure if other == axis else term)
    flux.append((energy + pressure) * along)
    speed = jnp.abs(along) + jnp.sqrt(GAMMA * pressure * inverse)
    return flux, speed


def normal_flux(parts, normal):
    density, energy = parts[0], parts[4]
    motion = [parts[1 + axis] / density for axis in range(3)]
    pressure = (GAMMA - 1.0) * (
        energy - 0.5 * (parts[1] * motion[0] + parts[2] * motion[1] + parts[3] * motion[2])
    )
    along = motion[0] * normal[0] + motion[1] * normal[1] + motion[2] * normal[2]
    flux = [density * along]
    for axis in range(3):
        flux.append(parts[1 + axis] * along + pressure * normal[axis])
    flux.append((energy + pressure) * along)
    speed = jnp.abs(along) + jnp.sqrt(GAMMA * pressure / density)
    return flux, speed


def split(columns):
    return [columns[16 * v : 16 * v + 16] for v in range(5)]


def rest_state():
    row = lax.broadcasted_iota(jnp.int32, (80, 128), 0)
    return jnp.where(row < 16, 1.0, jnp.where(row >= 64, 2.5, 0.0)).astype(jnp.float32)


def kernel(
    count,
    state_hbm,
    levels_ref,
    send_ref,
    partner_ref,
    mortar_ref,
    dir_ref,
    return_ref,
    source_ref,
    matrix_ref,
    out_ref,
    st,
    tr,
    snd,
    rcv,
    acc,
    own,
    spd,
    res,
    ftmp,
    mor,
    tab,
    rsnd,
    rrcv,
    pad,
    jmp,
    load_sem,
    send_sem,
    recv_sem,
    rsend_sem,
    rrecv_sem,
):
    me = lax.axis_index("dev")
    derivative = [[float(x) for x in row] for row in lobatto_tables()[0]]

    def peer_of(p):
        offset = jnp.where(p < 4, p + 1, 3 - p)
        return lax.rem(me + offset + count, count)

    barrier = pltpu.get_barrier_semaphore()
    for p in range(8):
        pl.semaphore_signal(barrier, inc=1, device_id=(peer_of(p),), device_id_type=MESH)
    loads = [
        pltpu.make_async_copy(
            state_hbm.at[:, :, pl.ds(128 * c, 128)], st.at[c], load_sem.at[c]
        )
        for c in range(TILES)
    ]
    for load in loads:
        load.start()

    lane = lax.broadcasted_iota(jnp.int32, (8, 128), 1)
    lane1 = lane[0:1]
    rest = rest_state()

    pad[...] = jnp.full((8, 128), 3072, jnp.int32)
    pad[0:5, 0:40] = mortar_ref[...]
    pad[5:6, 0:40] = dir_ref[...]
    pad[6:8, 0:32] = return_ref[...]
    packed = pad[...]
    by40 = pltpu.roll(packed, 40, axis=1)
    by80 = pltpu.roll(packed, 80, axis=1)
    entry = [
        jnp.where(
            lane1 < 40,
            packed[0:1],
            jnp.where(lane1 < 80, by40[1:2], jnp.where(lane1 < 120, by80[2:3], 3072)),
        ),
        jnp.where(lane1 < 40, packed[3:4], jnp.where(lane1 < 80, by40[4:5], 3072)),
    ]
    direction = [
        jnp.where(lane1 < 40, packed[5:6], jnp.where(lane1 < 80, by40[5:6], by80[5:6])),
        jnp.where(lane1 < 40, packed[5:6], by40[5:6]),
    ]
    by32 = pltpu.roll(packed, 32, axis=1)
    by64 = pltpu.roll(packed, 64, axis=1)
    by96 = pltpu.roll(packed, 96, axis=1)
    leaving = jnp.where(
        lane < 32, packed, jnp.where(lane < 64, by32, jnp.where(lane < 96, by64, by96))
    )[6:8]

    def placed(index):
        moved = jnp.where(index > 3072, index - 1, index)
        tile = jnp.where(index == 3072, -1, jnp.right_shift(moved, 7))
        return tile, jnp.bitwise_and(moved, 127)

    def wide(row, rows=80):
        return jnp.broadcast_to(row, (rows, 128))

    for load in loads:
        load.wait()

    def trace_step(c, carry):
        for v in range(5):
            tr[0, c, 16 * v : 16 * v + 16] = st[c, v, 0:16]
            tr[1, c, 16 * v : 16 * v + 16] = st[c, v, 48:64]
            for i in range(4):
                tr[2, c, 16 * v + 4 * i : 16 * v + 4 * i + 4] = st[c, v, 16 * i : 16 * i + 4]
                tr[3, c, 16 * v + 4 * i : 16 * v + 4 * i + 4] = st[c, v, 16 * i + 12 : 16 * i + 16]
            tr[4, c, 16 * v : 16 * v + 16] = st[c, v, pl.ds(0, 16, 4)]
            tr[5, c, 16 * v : 16 * v + 16] = st[c, v, pl.ds(3, 16, 4)]
        return carry

    lax.fori_loop(0, TILES, trace_step, 0)

    pl.semaphore_wait(barrier, 8)

    def trace_copy(p):
        return pltpu.make_async_remote_copy(
            src_ref=snd.at[p],
            dst_ref=rcv.at[p],
            send_sem=send_sem.at[p],
            recv_sem=recv_sem.at[p],
            device_id=(peer_of(p),),
            device_id_type=MESH,
        )

    def order(k):
        return lax.rem(k, 2) * 4 + lax.rem(4 - k // 2, 4)

    def send_step(k, carry):
        p = order(k)
        index = send_ref[pl.ds(p, 1), :]
        tile = wide(jnp.right_shift(index, 7))
        place = wide(jnp.bitwise_and(index, 127))
        value = rest
        for f in range(6):
            for c in range(TILES):
                value = jnp.where(tile == f * TILES + c, lanes_of(tr[f, c], place), value)
        snd[p] = value
        trace_copy(p).start()
        return carry

    lax.fori_loop(0, 8, send_step, 0)

    for m in range(2):
        tile, place = placed(entry[m])
        tile, place = wide(tile), wide(place)
        value = rest
        for f in range(4):
            for c in range(TILES):
                value = jnp.where(tile == f * TILES + c, lanes_of(tr[f, c], place), value)
        mor[m] = value

    row16 = lax.broadcasted_iota(jnp.int32, (16, 128), 0)
    second = jnp.right_shift(row16, 2)

    def by_row(shift):
        picks = [derivative[j][(j - shift) % 4] for j in range(4)]
        return jnp.where(
            second == 0,
            picks[0],
            jnp.where(second == 1, picks[1], jnp.where(second == 2, picks[2], picks[3])),
        ).astype(jnp.float32)

    weights = [by_row(shift) for shift in range(4)]

    def volume_step(c, carry):
        for i in range(4):
            rows = pl.ds(16 * i, 16)
            parts = [st[c, v, rows] for v in range(5)]
            inverse = 1.0 / parts[0]
            motion = [parts[1 + a] * inverse for a in range(3)]
            pressure = (GAMMA - 1.0) * (
                parts[4]
                - 0.5 * (parts[1] * motion[0] + parts[2] * motion[1] + parts[3] * motion[2])
            )
            for axis in range(3):
                flux = [parts[1 + axis]]
                for other in range(3):
                    term = parts[1 + other] * motion[axis]
                    flux.append(term + pressure if other == axis else term)
                flux.append((parts[4] + pressure) * motion[axis])
                for v in range(5):
                    if axis == 0:
                        ftmp[0, v, rows] = flux[v]
                    elif axis == 2:
                        ftmp[1, v, rows] = flux[v]
                    else:
                        total = weights[0] * flux[v]
                        for shift in range(1, 4):
                            total += weights[shift] * pltpu.roll(flux[v], 4 * shift, axis=0)
                        res[c, v, rows] = total
        for v in range(5):
            terms = [ftmp[0, v, 16 * i : 16 * i + 16] for i in range(4)]
            for a in range(4):
                total = res[c, v, 16 * a : 16 * a + 16]
                for i in range(4):
                    total += derivative[a][i] * terms[i]
                res[c, v, 16 * a : 16 * a + 16] = total
        for v in range(5):
            terms = [ftmp[1, v, pl.ds(k, 16, 4)] for k in range(4)]
            for a in range(4):
                total = res[c, v, pl.ds(a, 16, 4)]
                for k in range(4):
                    total += derivative[a][k] * terms[k]
                res[c, v, pl.ds(a, 16, 4)] = total
        return carry

    lax.fori_loop(0, TILES, volume_step, 0)

    def local_step(c, carry):
        span = pl.ds(pl.multiple_of(128 * c, 128), 128)
        for f in range(6):
            flux, speed = axis_flux(split(tr[f, c]), SIDE[f], 2.0 * (f % 2) - 1.0)
            for v in range(5):
                own[f, c, 16 * v : 16 * v + 16] = flux[v]
            spd[f, c] = speed
            tile, place = placed(partner_ref[f : f + 1, span])
            tile, place = wide(tile), wide(place)
            value = rest
            for t in range(TILES):
                value = jnp.where(
                    tile == (f ^ 1) * TILES + t, lanes_of(tr[f ^ 1, t], place), value
                )
            acc[f, c] = value
        return carry

    lax.fori_loop(0, TILES, local_step, 0)

    trace_copy(0).wait_recv()
    trace_copy(4).wait_recv()
    states = []
    for m in range(2):
        tile, place = placed(entry[m])
        tile, place = wide(tile), wide(place)
        value = mor[m]
        for p in (0, 4):
            value = jnp.where(tile == 24 + p, lanes_of(rcv[p], place), value)
        states.append(value)
    lane80 = wide(lane1)
    big = jnp.where(
        lane80 < 40,
        states[0],
        jnp.where(
            lane80 < 80,
            pltpu.roll(states[0], 40, axis=1),
            pltpu.roll(states[0], 80, axis=1),
        ),
    )
    near = jnp.dot(
        matrix_ref[0:320], big, precision=HIGHEST, preferred_element_type=jnp.float32
    )
    nears = [
        jnp.where(lane80 < 80, near[0:80], near[80:160]),
        jnp.where(lane80 < 40, near[160:240], near[240:320]),
    ]
    stars = []
    for m in range(2):
        normal = [
            wide(
                jnp.where(direction[m] == 2 * axis + 1, 1.0, 0.0)
                - jnp.where(direction[m] == 2 * axis, 1.0, 0.0),
                16,
            )
            for axis in range(3)
        ]
        inside, outside = split(nears[m]), split(states[m])
        inside_flux, inside_speed = normal_flux(inside, normal)
        outside_flux, outside_speed = normal_flux(outside, normal)
        half = 0.5 * jnp.maximum(inside_speed, outside_speed)
        stars.append(
            jnp.concatenate(
                [
                    0.5 * (inside_flux[v] + outside_flux[v]) - half * (outside[v] - inside[v])
                    for v in range(5)
                ],
                axis=0,
            )
        )
    home_a = jnp.dot(
        matrix_ref[320:480], stars[0], precision=HIGHEST, preferred_element_type=jnp.float32
    )
    home_b = jnp.dot(
        matrix_ref[480:640], stars[1], precision=HIGHEST, preferred_element_type=jnp.float32
    )
    together = (
        pltpu.roll(home_a[0:80], 88, axis=1)
        + pltpu.roll(home_a[80:160], 48, axis=1)
        + home_b[0:80]
        + pltpu.roll(home_b[80:160], 88, axis=1)
    )
    tab[0] = jnp.where(lane80 < 40, together, -stars[0])
    tab[1] = -stars[1]

    def return_copy(side):
        step = 1 - 2 * side
        return pltpu.make_async_remote_copy(
            src_ref=rsnd.at[side],
            dst_ref=rrcv.at[side],
            send_sem=rsend_sem.at[side],
            recv_sem=rrecv_sem.at[side],
            device_id=(lax.rem(me + step + count, count),),
            device_id_type=MESH,
        )

    quarter = jnp.right_shift(lane, 5)
    for side in range(2):
        index = wide(leaving[side : side + 1], 8)
        first = index < 120
        named = index < 200
        place = jnp.bitwise_and(jnp.where(first, index, index - 120), 127)
        for k in range(3):
            value = jnp.zeros((8, 128), jnp.float32)
            for b in range(4):
                g = 4 * k + b
                if g < 10:
                    rows = slice(8 * g, 8 * g + 8)
                    found = jnp.where(
                        first, lanes_of(tab[0, rows], place), lanes_of(tab[1, rows], place)
                    )
                    value = jnp.where((quarter == b) & named, found, value)
            rsnd[side, 8 * k : 8 * k + 8] = value
        return_copy(side).start()

    def arrive_step(k, carry):
        p = order(k)

        @pl.when(k >= 2)
        def _():
            trace_copy(p).wait_recv()

        def tile_step(c, inner):
            span = pl.ds(pl.multiple_of(128 * c, 128), 128)
            table = rcv[p]
            for f in range(6):
                tile, place = placed(partner_ref[f : f + 1, span])
                acc[f, c] = jnp.where(
                    wide(tile) == 24 + p, lanes_of(table, wide(place)), acc[f, c]
                )
            return inner

        lax.fori_loop(0, TILES, tile_step, 0)
        return carry

    lax.fori_loop(0, 8, arrive_step, 0)
    return_copy(0).wait_recv()
    return_copy(1).wait_recv()

    def final_step(c, carry):
        span = pl.ds(pl.multiple_of(128 * c, 128), 128)
        for f in range(6):
            here, there = tr[f, c], acc[f, c]
            inside, outside = split(here), split(there)
            flux, speed = axis_flux(outside, SIDE[f], 2.0 * (f % 2) - 1.0)
            half = 0.5 * jnp.maximum(spd[f, c], speed)
            jumps = [
                0.5 * (flux[v] - own[f, c, 16 * v : 16 * v + 16]) - half * (outside[v] - inside[v])
                for v in range(5)
            ]
            if f < 4:
                index = wide(source_ref[f : f + 1, span], 8)
                first, second_tile = index < 120, index < 200
                third = index < 233
                place = jnp.bitwise_and(jnp.where(first, index, index - 120), 127)
                back = jnp.bitwise_and(jnp.where(third, index - 201, index - 233), 31)
                backs = [back + 32 * b for b in range(4)]
                for v in range(5):
                    pieces = []
                    for g in (2 * v, 2 * v + 1):
                        rows = slice(8 * g, 8 * g + 8)
                        packs = slice(8 * (g // 4), 8 * (g // 4) + 8)
                        far = backs[g % 4]
                        mortar = jnp.where(
                            first,
                            lanes_of(tab[0, rows], place),
                            jnp.where(
                                second_tile,
                                lanes_of(tab[1, rows], place),
                                jnp.where(
                                    third,
                                    lanes_of(rrcv[0, packs], far),
                                    lanes_of(rrcv[1, packs], far),
                                ),
                            ),
                        )
                        half_rows = slice(8 * (g % 2), 8 * (g % 2) + 8)
                        pieces.append(
                            jnp.where(
                                index == 200, jumps[v][half_rows], mortar - own[f, c, rows]
                            )
                        )
                    jumps[v] = jnp.concatenate(pieces, axis=0)
            for v in range(5):
                lift = 6.0 * jumps[v]
                if f < 2:
                    res[c, v, 48 * f : 48 * f + 16] += lift
                elif f < 4:
                    jmp[v] = lift
                    for i in range(4):
                        at = 16 * i + 12 * (f - 2)
                        res[c, v, at : at + 4] += jmp[v, 4 * i : 4 * i + 4]
                else:
                    res[c, v, pl.ds(3 * (f - 4), 16, 4)] += lift
        scale = -jnp.exp2(levels_ref[0:1, span].astype(jnp.float32) + 1.0)
        for v in range(5):
            out_ref[v, :, span] = wide(scale, 64) * res[c, v]
        return carry

    lax.fori_loop(0, TILES, final_step, 0)

    for p in range(8):
        trace_copy(p).wait_send()
    for side in range(2):
        return_copy(side).wait_send()


def body(
    state, step_size, levels, send_faces, partner, mortar_in, mortar_dir, return_faces, flux_source
):


    count = lax.axis_size("dev")
    vmem = pl.BlockSpec(memory_space=pltpu.VMEM)
    f32 = jnp.float32
    residual = pl.pallas_call(
        functools.partial(kernel, count),
        out_shape=jax.ShapeDtypeStruct(state.shape, f32),
        in_specs=[pl.BlockSpec(memory_space=pl.ANY)] + [vmem] * 8,
        out_specs=vmem,
        scratch_shapes=[
            pltpu.VMEM((TILES, 5, 64, 128), f32),
            pltpu.VMEM((6, TILES, 80, 128), f32),
            pltpu.VMEM((8, 80, 128), f32),
            pltpu.VMEM((8, 80, 128), f32),
            pltpu.VMEM((6, TILES, 80, 128), f32),
            pltpu.VMEM((6, TILES, 80, 128), f32),
            pltpu.VMEM((6, TILES, 16, 128), f32),
            pltpu.VMEM((TILES, 5, 64, 128), f32),
            pltpu.VMEM((2, 5, 64, 128), f32),
            pltpu.VMEM((2, 80, 128), f32),
            pltpu.VMEM((2, 80, 128), f32),
            pltpu.VMEM((2, 24, 128), f32),
            pltpu.VMEM((2, 24, 128), f32),
            pltpu.VMEM((8, 128), jnp.int32),
            pltpu.VMEM((5, 16, 128), f32),
            pltpu.SemaphoreType.DMA((TILES,)),
            pltpu.SemaphoreType.DMA((8,)),
            pltpu.SemaphoreType.DMA((8,)),
            pltpu.SemaphoreType.DMA((2,)),
            pltpu.SemaphoreType.DMA((2,)),
        ],
        compiler_params=pltpu.CompilerParams(
            collective_id=0, has_side_effects=True, vmem_limit_bytes=24 * 1024 * 1024
        ),
        name="section",
    )(
        state,
        levels.reshape(1, -1),
        send_faces,
        partner,
        mortar_in,
        mortar_dir.reshape(1, -1),
        return_faces,
        flux_source,
        jnp.asarray(mortar_matrices()),
    )
    return step_size[0] * residual


def solution(mesh):
    placed = (
        P(None, None, "dev"),
        P(),
        P("dev"),
        P("dev", None),
        P(None, "dev"),
        P(None, "dev"),
        P("dev"),
        P("dev", None),
        P(None, "dev"),
    )
    return jax.shard_map(
        body, mesh=mesh, in_specs=placed, out_specs=P(None, None, "dev"), check_vma=False
    )
```

time: 191 us -> 32 us (0.17)
  the two profiles are of different devices: /device:TPU:0 before, /device:TPU:1 now
where the time goes in v1:
time: 32 us; the launch traced here: 31.6 us
  Pallas kernels  25.1 us (78%)
  local copies, waits for them, and re-layouts  4.85 us (15%)
  other arithmetic  0.89 us (3%)
  between operations  0.71 us (2%)
    pallas_call x1, Pallas kernels, body(): pl.pallas_call(functools.partial(kernel, count), out_shape=jax.ShapeDtype...  25.1 us
    unnamed x18, local copies, waits for them, and re-layouts  4.85 us
    mul x1, other arithmetic, body(): return step_size[0] * residual  0.89 us

profile of v1, /device:TPU:1, one launch (start us, length us, event | category | flops | bytes accessed | tf_op | source)
XLA Modules:
  0.0 31.6 jit_solution(10990166418786898559)
XLA Ops:
  0.0 0.0 copy-start.4
  0.7 0.0 copy-start.6
  0.7 0.0 copy-start.7
  0.7 0.0 copy-start.8
  0.7 0.0 copy-done.4
  0.7 0.6 %copy-done.6 = s32[512]{0:T(512)S(1)} copy-done((s32[512]{0:T(512)S(1)}, s32[512]{0:T(512)}, u32[]{:S(2)}) %copy-start.6) | copy-done | bytes 2072
  1.4 0.0 copy-done.7
  1.4 0.0 copy-done.8
  1.4 0.0 copy-start
  1.4 1.1 %copy-done = f32[5,64,512]{2,1,0:T(8,128)S(1)} copy-done((f32[5,64,512]{2,1,0:T(8,128)S(1)}, f32[5,64,512]{2,1,0:T(8,128)}, u32[]{:S(2)}) %copy-start) | copy-done | bytes 655384
  2.5 0.0 copy-start.1
  2.5 1.0 %copy-done.1 = f32[640,80]{1,0:T(8,128)S(1)} copy-done((f32[640,80]{1,0:T(8,128)S(1)}, f32[640,80]{1,0:T(8,128)}, u32[]{:S(2)}) %copy-start.1) | copy-done | bytes 204824
  3.4 0.0 copy-start.2
  3.4 0.7 %copy-done.2 = s32[6,512]{1,0:T(8,128)S(1)} copy-done((s32[6,512]{1,0:T(8,128)S(1)}, s32[6,512]{1,0:T(8,128)}, u32[]{:S(2)}) %copy-start.2) | copy-done | bytes 12312
  4.1 0.0 copy-start.3
  4.1 0.7 %copy-done.3 = s32[6,512]{1,0:T(8,128)S(1)} copy-done((s32[6,512]{1,0:T(8,128)S(1)}, s32[6,512]{1,0:T(8,128)}, u32[]{:S(2)}) %copy-start.3) | copy-done | bytes 12312
  4.9 0.0 copy-start.5
  4.9 0.7 %copy-done.5 = s32[5,40]{1,0:T(8,128)S(1)} copy-done((s32[5,40]{1,0:T(8,128)S(1)}, s32[5,40]{1,0:T(8,128)}, u32[]{:S(2)}) %copy-start.5) | copy-done | bytes 824
  5.6 25.1 %section.1 = f32[5,64,512]{2,1,0:T(8,128)S(1)} custom-call(f32[5,64,512]{2,1,0:T(8,128)S(1)} %copy-done, s32[1,512]{1,0:T(1,128)S(1)} %bitcast.4, s32[8,128]{1,0:T(8,128)S(1)} %copy-done.4, s32[6,512]{1,0:T(8,128)S(1)} %copy-done.2, s32[5,40]{1,0:T(8,128)S(1)} %copy-done.5, s32[1,40]{1,0:T(1,128)S(1)} %bitcast.5, s32[2,32]{1,0:T(2,128)S(1)} %copy-done.7, ...), custom_call_target="tpu_custom_call" | custom-call | tf_op jit(solution)/shard_map/section/pallas_call | solution.py:519
  30.7 0.9 %broadcast_multiply_fusion = f32[5,64,512]{2,1,0:T(8,128)} fusion(f32[5,64,512]{2,1,0:T(8,128)S(1)} %section.1, f32[]{:T(128)} %bitcast.3), kind=kLoop, calls=%fused_computation | loop fusion | flops 163840 | bytes 1310724 | tf_op jit(solution)/shard_map/mul | solution.py:561
Async XLA Ops:
  0.0 0.7 %copy-start.4 = (s32[8,128]{1,0:T(8,128)S(1)}, s32[8,128]{1,0:T(8,128)}, u32[]{:S(2)}) copy-start(s32[8,128]{1,0:T(8,128)} %send_ref.1) | copy-start | bytes 12292
  0.7 0.7 %copy-start.6 = (s32[512]{0:T(512)S(1)}, s32[512]{0:T(512)}, u32[]{:S(2)}) copy-start(s32[512]{0:T(512)} %param.12) | copy-start | bytes 6148
  0.7 0.7 %copy-start.7 = (s32[2,32]{1,0:T(2,128)S(1)}, s32[2,32]{1,0:T(2,128)}, u32[]{:S(2)}) copy-start(s32[2,32]{1,0:T(2,128)} %return_ref.1) | copy-start | bytes 772
  0.7 0.7 %copy-start.8 = (s32[40]{0:T(128)S(1)}, s32[40]{0:T(128)}, u32[]{:S(2)}) copy-start(s32[40]{0:T(128)} %param.16) | copy-start | bytes 484
  1.4 1.1 %copy-start = (f32[5,64,512]{2,1,0:T(8,128)S(1)}, f32[5,64,512]{2,1,0:T(8,128)}, u32[]{:S(2)}) copy-start(f32[5,64,512]{2,1,0:T(8,128)} %state_hbm.1) | copy-start | bytes 1966084
  2.5 1.0 %copy-start.1 = (f32[640,80]{1,0:T(8,128)S(1)}, f32[640,80]{1,0:T(8,128)}, u32[]{:S(2)}) copy-start(f32[640,80]{1,0:T(8,128)} %constant.2.clone.matrix_ref) | copy-start | bytes 614404
  3.4 0.7 %copy-start.2 = (s32[6,512]{1,0:T(8,128)S(1)}, s32[6,512]{1,0:T(8,128)}, u32[]{:S(2)}) copy-start(s32[6,512]{1,0:T(8,128)} %partner_ref.1) | copy-start | bytes 36868
  4.1 0.7 %copy-start.3 = (s32[6,512]{1,0:T(8,128)S(1)}, s32[6,512]{1,0:T(8,128)}, u32[]{:S(2)}) copy-start(s32[6,512]{1,0:T(8,128)} %source_ref.1) | copy-start | bytes 36868
  4.9 0.7 %copy-start.5 = (s32[5,40]{1,0:T(8,128)S(1)}, s32[5,40]{1,0:T(8,128)}, u32[]{:S(2)}) copy-start(s32[5,40]{1,0:T(8,128)} %mortar_ref.1) | copy-start | bytes 2404

commit v2 on v1

--- a/solution.py
+++ b/solution.py
@@ -1,4 +1,5 @@
 import functools
+
 import jax
 import jax.numpy as jnp
 import numpy as np
@@ -103,6 +104,15 @@
 def kernel(
     count,
     state_hbm,
+    levels_hbm,
+    send_hbm,
+    partner_hbm,
+    mortar_hbm,
+    dir_hbm,
+    return_hbm,
+    source_hbm,
+    matrix_hbm,
+    out_ref,
     levels_ref,
     send_ref,
     partner_ref,
@@ -111,7 +121,6 @@
     return_ref,
     source_ref,
     matrix_ref,
-    out_ref,
     st,
     tr,
     snd,
@@ -126,8 +135,10 @@
     rsnd,
     rrcv,
     pad,
-    jmp,
+    lift_j,
+    lift_k,
     load_sem,
+    small_sem,
     send_sem,
     recv_sem,
     rsend_sem,
@@ -143,19 +154,164 @@
     barrier = pltpu.get_barrier_semaphore()
     for p in range(8):
         pl.semaphore_signal(barrier, inc=1, device_id=(peer_of(p),), device_id_type=MESH)
-    loads = [
-        pltpu.make_async_copy(
-            state_hbm.at[:, :, pl.ds(128 * c, 128)], st.at[c], load_sem.at[c]
+
+    def load_of(c):
+        span = pl.ds(pl.multiple_of(128 * c, 128), 128)
+        return pltpu.make_async_copy(state_hbm.at[:, :, span], st.at[c], load_sem.at[c])
+
+    for c in range(TILES):
+        load_of(c).start()
+    small = [
+        pltpu.make_async_copy(source, target, small_sem.at[n])
+        for n, (source, target) in enumerate(
+            (
+                (send_hbm, send_ref),
+                (mortar_hbm, mortar_ref),
+                (dir_hbm, dir_ref),
+                (return_hbm, return_ref),
+                (partner_hbm, partner_ref),
+                (source_hbm, source_ref),
+                (levels_hbm, levels_ref),
+                (matrix_hbm, matrix_ref),
+            )
         )
-        for c in range(TILES)
     ]
-    for load in loads:
+    for load in small:
         load.start()
 
     lane = lax.broadcasted_iota(jnp.int32, (8, 128), 1)
     lane1 = lane[0:1]
     rest = rest_state()
 
+    def placed(index):
+        moved = jnp.where(index > 3072, index - 1, index)
+        tile = jnp.where(index == 3072, -1, jnp.right_shift(moved, 7))
+        return tile, jnp.bitwise_and(moved, 127)
+
+    def wide(row, rows=80):
+        return jnp.broadcast_to(row, (rows, 128))
+
+    def trace_step(c, carry):
+        load_of(c).wait()
+        for v in range(5):
+            tr[0, c, 16 * v : 16 * v + 16] = st[c, v, 0:16]
+            tr[1, c, 16 * v : 16 * v + 16] = st[c, v, 48:64]
+            for i in range(4):
+                tr[2, c, 16 * v + 4 * i : 16 * v + 4 * i + 4] = st[c, v, 16 * i : 16 * i + 4]
+                tr[3, c, 16 * v + 4 * i : 16 * v + 4 * i + 4] = st[c, v, 16 * i + 12 : 16 * i + 16]
+            tr[4, c, 16 * v : 16 * v + 16] = st[c, v, pl.ds(0, 16, 4)]
+            tr[5, c, 16 * v : 16 * v + 16] = st[c, v, pl.ds(3, 16, 4)]
+        return carry
+
+    lax.fori_loop(0, TILES, trace_step, 0)
+
+
+    def trace_copy(p):
+        return pltpu.make_async_remote_copy(
+            src_ref=snd.at[p],
+            dst_ref=rcv.at[p],
+            send_sem=send_sem.at[p],
+            recv_sem=recv_sem.at[p],
+            device_id=(peer_of(p),),
+            device_id_type=MESH,
+        )
+
+    def order(k):
+        return lax.rem(k, 2) * 4 + lax.rem(4 - k // 2, 4)
+
+    row16 = lax.broadcasted_iota(jnp.int32, (16, 128), 0)
+    second = jnp.right_shift(row16, 2)
+
+    def by_row(shift):
+        picks = [derivative[j][(j - shift) % 4] for j in range(4)]
+        return jnp.where(
+            second == 0,
+            picks[0],
+            jnp.where(second == 1, picks[1], jnp.where(second == 2, picks[2], picks[3])),
+        ).astype(jnp.float32)
+
+    weights = [by_row(shift) for shift in range(4)]
+
+    def fluxes_of(c):
+        for i in range(4):
+            rows = pl.ds(16 * i, 16)
+            parts = [st[c, v, rows] for v in range(5)]
+            inverse = 1.0 / parts[0]
+            motion = [parts[1 + a] * inverse for a in range(3)]
+            pressure = (GAMMA - 1.0) * (
+                parts[4]
+                - 0.5 * (parts[1] * motion[0] + parts[2] * motion[1] + parts[3] * motion[2])
+            )
+            for axis in range(3):
+                flux = [parts[1 + axis]]
+                for other in range(3):
+                    term = parts[1 + other] * motion[axis]
+                    flux.append(term + pressure if other == axis else term)
+                flux.append((parts[4] + pressure) * motion[axis])
+                for v in range(5):
+                    if axis == 0:
+                        ftmp[0, v, rows] = flux[v]
+                    elif axis == 2:
+                        ftmp[1, v, rows] = flux[v]
+                    else:
+                        total = weights[0] * flux[v]
+                        for shift in range(1, 4):
+                            total += weights[shift] * pltpu.roll(flux[v], 4 * shift, axis=0)
+                        res[c, v, rows] = total
+
+    def slopes_of(c):
+        for v in range(5):
+            terms = [ftmp[0, v, 16 * i : 16 * i + 16] for i in range(4)]
+            for a in range(4):
+                total = res[c, v, 16 * a : 16 * a + 16]
+                for i in range(4):
+                    total += derivative[a][i] * terms[i]
+                res[c, v, 16 * a : 16 * a + 16] = total
+        for v in range(5):
+            terms = [ftmp[1, v, pl.ds(k, 16, 4)] for k in range(4)]
+            for a in range(4):
+                total = res[c, v, pl.ds(a, 16, 4)]
+                for k in range(4):
+                    total += derivative[a][k] * terms[k]
+                res[c, v, pl.ds(a, 16, 4)] = total
+
+    def own_fluxes_of(c):
+        for f in range(6):
+            flux, speed = axis_flux(split(tr[f, c]), SIDE[f], 2.0 * (f % 2) - 1.0)
+            for v in range(5):
+                own[f, c, 16 * v : 16 * v + 16] = flux[v]
+            spd[f, c] = speed
+
+    def outgoing(p):
+        index = send_ref[pl.ds(p, 1), :]
+        tile = wide(jnp.right_shift(index, 7))
+        place = wide(jnp.bitwise_and(index, 127))
+        value = rest
+        for f in range(6):
+            for c in range(TILES):
+                value = jnp.where(tile == f * TILES + c, lanes_of(tr[f, c], place), value)
+        snd[p] = value
+
+    def send_step(c, carry):
+        p = lax.rem(4 - c, 4)
+        outgoing(p)
+        fluxes_of(c)
+        outgoing(p + 4)
+        slopes_of(c)
+        own_fluxes_of(c)
+        for v in range(5):
+            lift_j[c, v] = jnp.zeros((64, 128), jnp.float32)
+            lift_k[c, v] = jnp.zeros((64, 128), jnp.float32)
+        return carry
+
+    small[0].wait()
+    lax.fori_loop(0, TILES, send_step, 0)
+    pl.semaphore_wait(barrier, 8)
+    for p in (0, 4):
+        trace_copy(p).start()
+
+    for n in (1, 2, 3):
+        small[n].wait()
     pad[...] = jnp.full((8, 128), 3072, jnp.int32)
     pad[0:5, 0:40] = mortar_ref[...]
     pad[5:6, 0:40] = dir_ref[...]
@@ -182,60 +338,6 @@
         lane < 32, packed, jnp.where(lane < 64, by32, jnp.where(lane < 96, by64, by96))
     )[6:8]
 
-    def placed(index):
-        moved = jnp.where(index > 3072, index - 1, index)
-        tile = jnp.where(index == 3072, -1, jnp.right_shift(moved, 7))
-        return tile, jnp.bitwise_and(moved, 127)
-
-    def wide(row, rows=80):
-        return jnp.broadcast_to(row, (rows, 128))
-
-    for load in loads:
-        load.wait()
-
-    def trace_step(c, carry):
-        for v in range(5):
-            tr[0, c, 16 * v : 16 * v + 16] = st[c, v, 0:16]
-            tr[1, c, 16 * v : 16 * v + 16] = st[c, v, 48:64]
-            for i in range(4):
-                tr[2, c, 16 * v + 4 * i : 16 * v + 4 * i + 4] = st[c, v, 16 * i : 16 * i + 4]
-                tr[3, c, 16 * v + 4 * i : 16 * v + 4 * i + 4] = st[c, v, 16 * i + 12 : 16 * i + 16]
-            tr[4, c, 16 * v : 16 * v + 16] = st[c, v, pl.ds(0, 16, 4)]
-            tr[5, c, 16 * v : 16 * v + 16] = st[c, v, pl.ds(3, 16, 4)]
-        return carry
-
-    lax.fori_loop(0, TILES, trace_step, 0)
-
-    pl.semaphore_wait(barrier, 8)
-
-    def trace_copy(p):
-        return pltpu.make_async_remote_copy(
-            src_ref=snd.at[p],
-            dst_ref=rcv.at[p],
-            send_sem=send_sem.at[p],
-            recv_sem=recv_sem.at[p],
-            device_id=(peer_of(p),),
-            device_id_type=MESH,
-        )
-
-    def order(k):
-        return lax.rem(k, 2) * 4 + lax.rem(4 - k // 2, 4)
-
-    def send_step(k, carry):
-        p = order(k)
-        index = send_ref[pl.ds(p, 1), :]
-        tile = wide(jnp.right_shift(index, 7))
-        place = wide(jnp.bitwise_and(index, 127))
-        value = rest
-        for f in range(6):
-            for c in range(TILES):
-                value = jnp.where(tile == f * TILES + c, lanes_of(tr[f, c], place), value)
-        snd[p] = value
-        trace_copy(p).start()
-        return carry
-
-    lax.fori_loop(0, 8, send_step, 0)
-
     for m in range(2):
         tile, place = placed(entry[m])
         tile, place = wide(tile), wide(place)
@@ -245,84 +347,11 @@
                 value = jnp.where(tile == f * TILES + c, lanes_of(tr[f, c], place), value)
         mor[m] = value
 
-    row16 = lax.broadcasted_iota(jnp.int32, (16, 128), 0)
-    second = jnp.right_shift(row16, 2)
-
-    def by_row(shift):
-        picks = [derivative[j][(j - shift) % 4] for j in range(4)]
-        return jnp.where(
-            second == 0,
-            picks[0],
-            jnp.where(second == 1, picks[1], jnp.where(second == 2, picks[2], picks[3])),
-        ).astype(jnp.float32)
-
-    weights = [by_row(shift) for shift in range(4)]
-
-    def volume_step(c, carry):
-        for i in range(4):
-            rows = pl.ds(16 * i, 16)
-            parts = [st[c, v, rows] for v in range(5)]
-            inverse = 1.0 / parts[0]
-            motion = [parts[1 + a] * inverse for a in range(3)]
-            pressure = (GAMMA - 1.0) * (
-                parts[4]
-                - 0.5 * (parts[1] * motion[0] + parts[2] * motion[1] + parts[3] * motion[2])
-            )
-            for axis in range(3):
-                flux = [parts[1 + axis]]
-                for other in range(3):
-                    term = parts[1 + other] * motion[axis]
-                    flux.append(term + pressure if other == axis else term)
-                flux.append((parts[4] + pressure) * motion[axis])
-                for v in range(5):
-                    if axis == 0:
-                        ftmp[0, v, rows] = flux[v]
-                    elif axis == 2:
-                        ftmp[1, v, rows] = flux[v]
-                    else:
-                        total = weights[0] * flux[v]
-                        for shift in range(1, 4):
-                            total += weights[shift] * pltpu.roll(flux[v], 4 * shift, axis=0)
-                        res[c, v, rows] = total
-        for v in range(5):
-            terms = [ftmp[0, v, 16 * i : 16 * i + 16] for i in range(4)]
-            for a in range(4):
-                total = res[c, v, 16 * a : 16 * a + 16]
-                for i in range(4):
-                    total += derivative[a][i] * terms[i]
-                res[c, v, 16 * a : 16 * a + 16] = total
-        for v in range(5):
-            terms = [ftmp[1, v, pl.ds(k, 16, 4)] for k in range(4)]
-            for a in range(4):
-                total = res[c, v, pl.ds(a, 16, 4)]
-                for k in range(4):
-                    total += derivative[a][k] * terms[k]
-                res[c, v, pl.ds(a, 16, 4)] = total
-        return carry
-
-    lax.fori_loop(0, TILES, volume_step, 0)
-
-    def local_step(c, carry):
-        span = pl.ds(pl.multiple_of(128 * c, 128), 128)
-        for f in range(6):
-            flux, speed = axis_flux(split(tr[f, c]), SIDE[f], 2.0 * (f % 2) - 1.0)
-            for v in range(5):
-                own[f, c, 16 * v : 16 * v + 16] = flux[v]
-            spd[f, c] = speed
-            tile, place = placed(partner_ref[f : f + 1, span])
-            tile, place = wide(tile), wide(place)
-            value = rest
-            for t in range(TILES):
-                value = jnp.where(
-                    tile == (f ^ 1) * TILES + t, lanes_of(tr[f ^ 1, t], place), value
-                )
-            acc[f, c] = value
-        return carry
-
-    lax.fori_loop(0, TILES, local_step, 0)
-
+    for p in (3, 7, 2, 6, 1, 5):
+        trace_copy(p).start()
     trace_copy(0).wait_recv()
     trace_copy(4).wait_recv()
+    small[7].wait()
     states = []
     for m in range(2):
         tile, place = placed(entry[m])
@@ -416,32 +445,50 @@
             rsnd[side, 8 * k : 8 * k + 8] = value
         return_copy(side).start()
 
+    small[4].wait()
+
+    def local_step(c, carry):
+        span = pl.ds(pl.multiple_of(128 * c, 128), 128)
+        for f in range(6):
+            tile, place = placed(partner_ref[f : f + 1, span])
+            tile, place = wide(tile), wide(place)
+            value = rest
+            for t in range(TILES):
+                value = jnp.where(
+                    tile == (f ^ 1) * TILES + t, lanes_of(tr[f ^ 1, t], place), value
+                )
+            acc[f, c] = value
+        return carry
+
+    lax.fori_loop(0, TILES, local_step, 0)
+
     def arrive_step(k, carry):
-        p = order(k)
-
-        @pl.when(k >= 2)
+        p = lax.rem(4 - k, 4)
+
+        @pl.when(k >= 1)
         def _():
             trace_copy(p).wait_recv()
-
-        def tile_step(c, inner):
-            span = pl.ds(pl.multiple_of(128 * c, 128), 128)
-            table = rcv[p]
+            trace_copy(p + 4).wait_recv()
+
+        for c in range(TILES):
             for f in range(6):
-                tile, place = placed(partner_ref[f : f + 1, span])
-                acc[f, c] = jnp.where(
-                    wide(tile) == 24 + p, lanes_of(table, wide(place)), acc[f, c]
-                )
-            return inner
-
-        lax.fori_loop(0, TILES, tile_step, 0)
+                tile, place = placed(partner_ref[f : f + 1, 128 * c : 128 * c + 128])
+                tile, place = wide(tile), wide(place)
+                value = acc[f, c]
+                for q in (p, p + 4):
+                    value = jnp.where(tile == 24 + q, lanes_of(rcv[q], place), value)
+                acc[f, c] = value
         return carry
 
-    lax.fori_loop(0, 8, arrive_step, 0)
+    lax.fori_loop(0, 4, arrive_step, 0)
     return_copy(0).wait_recv()
     return_copy(1).wait_recv()
-
-    def final_step(c, carry):
-        span = pl.ds(pl.multiple_of(128 * c, 128), 128)
+    small[5].wait()
+    small[6].wait()
+
+    for c in range(TILES):
+        span = slice(128 * c, 128 * c + 128)
+        ends = [[None] * 5, [None] * 5]
         for f in range(6):
             here, there = tr[f, c], acc[f, c]
             inside, outside = split(here), split(there)
@@ -485,22 +532,22 @@
                         )
                     jumps[v] = jnp.concatenate(pieces, axis=0)
             for v in range(5):
-                lift = 6.0 * jumps[v]
                 if f < 2:
-                    res[c, v, 48 * f : 48 * f + 16] += lift
+                    ends[f][v] = jumps[v]
                 elif f < 4:
-                    jmp[v] = lift
                     for i in range(4):
                         at = 16 * i + 12 * (f - 2)
-                        res[c, v, at : at + 4] += jmp[v, 4 * i : 4 * i + 4]
+                        lift_j[c, v, at : at + 4] = jumps[v][4 * i : 4 * i + 4]
                 else:
-                    res[c, v, pl.ds(3 * (f - 4), 16, 4)] += lift
+                    lift_k[c, v, pl.ds(3 * (f - 4), 16, 4)] = jumps[v]
         scale = -jnp.exp2(levels_ref[0:1, span].astype(jnp.float32) + 1.0)
         for v in range(5):
-            out_ref[v, :, span] = wide(scale, 64) * res[c, v]
-        return carry
-
-    lax.fori_loop(0, TILES, final_step, 0)
+            for i in range(4):
+                rows = slice(16 * i, 16 * i + 16)
+                lift = lift_j[c, v, rows] + lift_k[c, v, rows]
+                if i in (0, 3):
+                    lift += ends[i // 3][v]
+                out_ref[v, rows, span] = wide(scale, 16) * (res[c, v, rows] + 6.0 * lift)
 
     for p in range(8):
         trace_copy(p).wait_send()
@@ -519,9 +566,17 @@
     residual = pl.pallas_call(
         functools.partial(kernel, count),
         out_shape=jax.ShapeDtypeStruct(state.shape, f32),
-        in_specs=[pl.BlockSpec(memory_space=pl.ANY)] + [vmem] * 8,
+        in_specs=[pl.BlockSpec(memory_space=pltpu.HBM)] * 9,
         out_specs=vmem,
         scratch_shapes=[
+            pltpu.VMEM((1, 512), jnp.int32),
+            pltpu.VMEM((8, 128), jnp.int32),
+            pltpu.VMEM((6, 512), jnp.int32),
+            pltpu.VMEM((5, 40), jnp.int32),
+            pltpu.VMEM((1, 40), jnp.int32),
+            pltpu.VMEM((2, 32), jnp.int32),
+            pltpu.VMEM((6, 512), jnp.int32),
+            pltpu.VMEM((640, 80), f32),
             pltpu.VMEM((TILES, 5, 64, 128), f32),
             pltpu.VMEM((6, TILES, 80, 128), f32),
             pltpu.VMEM((8, 80, 128), f32),
@@ -536,8 +591,10 @@
             pltpu.VMEM((2, 24, 128), f32),
             pltpu.VMEM((2, 24, 128), f32),
             pltpu.VMEM((8, 128), jnp.int32),
-            pltpu.VMEM((5, 16, 128), f32),
+            pltpu.VMEM((TILES, 5, 64, 128), f32),
+            pltpu.VMEM((TILES, 5, 64, 128), f32),
             pltpu.SemaphoreType.DMA((TILES,)),
+            pltpu.SemaphoreType.DMA((8,)),
             pltpu.SemaphoreType.DMA((8,)),
             pltpu.SemaphoreType.DMA((8,)),
             pltpu.SemaphoreType.DMA((2,)),
@@ -548,15 +605,20 @@
         ),
         name="section",
     )(
-        state,
-        levels.reshape(1, -1),
-        send_faces,
-        partner,
-        mortar_in,
-        mortar_dir.reshape(1, -1),
-        return_faces,
-        flux_source,
-        jnp.asarray(mortar_matrices()),
+        *(
+            pltpu.with_memory_space_constraint(array, pltpu.HBM)
+            for array in (
+                state,
+                levels.reshape(1, -1),
+                send_faces,
+                partner,
+                mortar_in,
+                mortar_dir.reshape(1, -1),
+                return_faces,
+                flux_source,
+                jnp.asarray(mortar_matrices()),
+            )
+        )
     )
     return step_size[0] * residual
 

time: 32 us -> 24.9 us (0.78)
  the two profiles are of different devices: /device:TPU:1 before, /device:TPU:0 now
where the time goes in v2:
time: 24.9 us; the launch traced here: 24.8 us
  Pallas kernels  23.2 us (93%)
  other arithmetic  0.89 us (4%)
  between operations  0.66 us (3%)
    pallas_call x1, Pallas kernels, body(): pl.pallas_call(functools.partial(kernel, count), out_shape=jax.ShapeDtype...  23.2 us
    mul x1, other arithmetic, body(): return step_size[0] * residual  0.89 us

profile of v2, /device:TPU:0, one launch (start us, length us, event | category | flops | bytes accessed | tf_op | source)
XLA Modules:
  0.0 24.8 jit_solution(4169582302569765315)
XLA Ops:
  0.7 23.2 %section.1 = f32[5,64,512]{2,1,0:T(8,128)S(1)} custom-call(f32[5,64,512]{2,1,0:T(8,128)} %state_hbm.1, s32[1,512]{1,0:T(1,128)} %bitcast.4, s32[8,128]{1,0:T(8,128)} %send_hbm.1, s32[6,512]{1,0:T(8,128)} %partner_hbm.1, s32[5,40]{1,0:T(8,128)} %mortar_hbm.1, s32[1,40]{1,0:T(1,128)} %bitcast.5, s32[2,32]{1,0:T(2,128)} %return_hbm.1, s32[6,512]{1,0:T(8,128)} %source_hbm.1, ...), custom_call_target="tpu_custom_call" | custom-call | tf_op jit(solution)/shard_map/section/pallas_call | solution.py:566
  23.9 0.9 %broadcast_multiply_fusion = f32[5,64,512]{2,1,0:T(8,128)} fusion(f32[5,64,512]{2,1,0:T(8,128)S(1)} %section.1, f32[]{:T(128)} %bitcast.3), kind=kLoop, calls=%fused_computation | loop fusion | flops 163840 | bytes 1310724 | tf_op jit(solution)/shard_map/mul | solution.py:623

commit v3 on v2

--- a/solution.py
+++ b/solution.py
@@ -112,29 +112,29 @@
     return_hbm,
     source_hbm,
     matrix_hbm,
-    out_ref,
+    res,
+    own,
+    rrcv,
+    source_ref,
     levels_ref,
     send_ref,
     partner_ref,
     mortar_ref,
     dir_ref,
     return_ref,
-    source_ref,
     matrix_ref,
     st,
     tr,
     snd,
     rcv,
     acc,
-    own,
     spd,
-    res,
     ftmp,
     mor,
     tab,
     rsnd,
-    rrcv,
     pad,
+    hang,
     lift_j,
     lift_k,
     load_sem,
@@ -307,7 +307,7 @@
     small[0].wait()
     lax.fori_loop(0, TILES, send_step, 0)
     pl.semaphore_wait(barrier, 8)
-    for p in (0, 4):
+    for p in (4, 0):
         trace_copy(p).start()
 
     for n in (1, 2, 3):
@@ -349,6 +349,23 @@
 
     for p in (3, 7, 2, 6, 1, 5):
         trace_copy(p).start()
+    small[4].wait()
+
+    def local_step(c, carry):
+        span = pl.ds(pl.multiple_of(128 * c, 128), 128)
+        for f in range(6):
+            tile, place = placed(partner_ref[f : f + 1, span])
+            tile, place = wide(tile), wide(place)
+            value = rest
+            for t in range(TILES):
+                value = jnp.where(
+                    tile == (f ^ 1) * TILES + t, lanes_of(tr[f ^ 1, t], place), value
+                )
+            acc[f, c] = value
+        return carry
+
+    lax.fori_loop(0, TILES, local_step, 0)
+
     trace_copy(0).wait_recv()
     trace_copy(4).wait_recv()
     small[7].wait()
@@ -445,22 +462,19 @@
             rsnd[side, 8 * k : 8 * k + 8] = value
         return_copy(side).start()
 
-    small[4].wait()
-
-    def local_step(c, carry):
+    small[5].wait()
+
+    def hang_step(c, carry):
         span = pl.ds(pl.multiple_of(128 * c, 128), 128)
-        for f in range(6):
-            tile, place = placed(partner_ref[f : f + 1, span])
-            tile, place = wide(tile), wide(place)
-            value = rest
-            for t in range(TILES):
-                value = jnp.where(
-                    tile == (f ^ 1) * TILES + t, lanes_of(tr[f ^ 1, t], place), value
-                )
-            acc[f, c] = value
+        for f in range(4):
+            index = wide(source_ref[f : f + 1, span])
+            first = index < 120
+            place = jnp.bitwise_and(jnp.where(first, index, index - 120), 127)
+            found = jnp.where(first, lanes_of(tab[0], place), lanes_of(tab[1], place))
+            hang[f, c] = jnp.where(index < 200, found - own[f, c], 0.0)
         return carry
 
-    lax.fori_loop(0, TILES, local_step, 0)
+    lax.fori_loop(0, TILES, hang_step, 0)
 
     def arrive_step(k, carry):
         p = lax.rem(4 - k, 4)
@@ -481,9 +495,6 @@
         return carry
 
     lax.fori_loop(0, 4, arrive_step, 0)
-    return_copy(0).wait_recv()
-    return_copy(1).wait_recv()
-    small[5].wait()
     small[6].wait()
 
     for c in range(TILES):
@@ -499,38 +510,9 @@
                 for v in range(5)
             ]
             if f < 4:
-                index = wide(source_ref[f : f + 1, span], 8)
-                first, second_tile = index < 120, index < 200
-                third = index < 233
-                place = jnp.bitwise_and(jnp.where(first, index, index - 120), 127)
-                back = jnp.bitwise_and(jnp.where(third, index - 201, index - 233), 31)
-                backs = [back + 32 * b for b in range(4)]
+                plain = wide(source_ref[f : f + 1, span], 16) == 200
                 for v in range(5):
-                    pieces = []
-                    for g in (2 * v, 2 * v + 1):
-                        rows = slice(8 * g, 8 * g + 8)
-                        packs = slice(8 * (g // 4), 8 * (g // 4) + 8)
-                        far = backs[g % 4]
-                        mortar = jnp.where(
-                            first,
-                            lanes_of(tab[0, rows], place),
-                            jnp.where(
-                                second_tile,
-                                lanes_of(tab[1, rows], place),
-                                jnp.where(
-                                    third,
-                                    lanes_of(rrcv[0, packs], far),
-                                    lanes_of(rrcv[1, packs], far),
-                                ),
-                            ),
-                        )
-                        half_rows = slice(8 * (g % 2), 8 * (g % 2) + 8)
-                        pieces.append(
-                            jnp.where(
-                                index == 200, jumps[v][half_rows], mortar - own[f, c, rows]
-                            )
-                        )
-                    jumps[v] = jnp.concatenate(pieces, axis=0)
+                    jumps[v] = jnp.where(plain, jumps[v], hang[f, c, 16 * v : 16 * v + 16])
             for v in range(5):
                 if f < 2:
                     ends[f][v] = jumps[v]
@@ -540,21 +522,84 @@
                         lift_j[c, v, at : at + 4] = jumps[v][4 * i : 4 * i + 4]
                 else:
                     lift_k[c, v, pl.ds(3 * (f - 4), 16, 4)] = jumps[v]
-        scale = -jnp.exp2(levels_ref[0:1, span].astype(jnp.float32) + 1.0)
         for v in range(5):
             for i in range(4):
                 rows = slice(16 * i, 16 * i + 16)
                 lift = lift_j[c, v, rows] + lift_k[c, v, rows]
                 if i in (0, 3):
                     lift += ends[i // 3][v]
-                out_ref[v, rows, span] = wide(scale, 16) * (res[c, v, rows] + 6.0 * lift)
-
+                res[c, v, rows] += 6.0 * lift
+
+    return_copy(0).wait_recv()
+    return_copy(1).wait_recv()
     for p in range(8):
         trace_copy(p).wait_send()
     for side in range(2):
         return_copy(side).wait_send()
 
 
+def close_kernel(
+    res,
+    own,
+    rrcv,
+    source_ref,
+    levels_ref,
+    step_ref,
+    out_hbm,
+    done,
+    lift_j,
+    out_sem,
+):
+    def wide(row, rows):
+        return jnp.broadcast_to(row, (rows, 128))
+
+    copies = []
+    for v in range(5):
+        lift_j[v] = jnp.zeros((64, 128), jnp.float32)
+    for c in range(TILES):
+        span = slice(128 * c, 128 * c + 128)
+        ends = [[None] * 5, [None] * 5]
+        for f in range(4):
+            index = wide(source_ref[f : f + 1, span], 8)
+            near_side, named = index < 233, index > 200
+            back = jnp.bitwise_and(jnp.where(near_side, index - 201, index - 233), 31)
+            backs = [back + 32 * b for b in range(4)]
+            for v in range(5):
+                pieces = []
+                for g in (2 * v, 2 * v + 1):
+                    packs = slice(8 * (g // 4), 8 * (g // 4) + 8)
+                    far = backs[g % 4]
+                    came = jnp.where(
+                        near_side,
+                        lanes_of(rrcv[0, packs], far),
+                        lanes_of(rrcv[1, packs], far),
+                    )
+                    pieces.append(
+                        jnp.where(named, came - own[f, c, 8 * g : 8 * g + 8], 0.0)
+                    )
+                if f < 2:
+                    ends[f][v] = jnp.concatenate(pieces, axis=0)
+                else:
+                    for i in range(4):
+                        at = 16 * i + 12 * (f - 2)
+                        half_rows = slice(4 * (i % 2), 4 * (i % 2) + 4)
+                        lift_j[v, at : at + 4] = pieces[i // 2][half_rows]
+        scale = -step_ref[0] * jnp.exp2(levels_ref[0:1, span].astype(jnp.float32) + 1.0)
+        for v in range(5):
+            for i in range(4):
+                rows = slice(16 * i, 16 * i + 16)
+                lift = lift_j[v, rows]
+                if i in (0, 3):
+                    lift += ends[i // 3][v]
+                done[c, v, rows] = wide(scale, 16) * (res[c, v, rows] + 6.0 * lift)
+        copies.append(
+            pltpu.make_async_copy(done.at[c], out_hbm.at[:, :, span], out_sem.at[c])
+        )
+        copies[c].start()
+    for copy in copies:
+        copy.wait()
+
+
 def body(
     state, step_size, levels, send_faces, partner, mortar_in, mortar_dir, return_faces, flux_source
 ):
@@ -563,34 +608,37 @@
     count = lax.axis_size("dev")
     vmem = pl.BlockSpec(memory_space=pltpu.VMEM)
     f32 = jnp.float32
-    residual = pl.pallas_call(
+    kept = (
+        pltpu.VMEM((TILES, 5, 64, 128), f32),
+        pltpu.VMEM((6, TILES, 80, 128), f32),
+        pltpu.VMEM((2, 24, 128), f32),
+        pltpu.VMEM((6, 512), jnp.int32),
+        pltpu.VMEM((1, 512), jnp.int32),
+    )
+    parts = pl.pallas_call(
         functools.partial(kernel, count),
-        out_shape=jax.ShapeDtypeStruct(state.shape, f32),
+        out_shape=kept,
         in_specs=[pl.BlockSpec(memory_space=pltpu.HBM)] * 9,
-        out_specs=vmem,
+        out_specs=(vmem,) * 5,
         scratch_shapes=[
-            pltpu.VMEM((1, 512), jnp.int32),
             pltpu.VMEM((8, 128), jnp.int32),
             pltpu.VMEM((6, 512), jnp.int32),
             pltpu.VMEM((5, 40), jnp.int32),
             pltpu.VMEM((1, 40), jnp.int32),
             pltpu.VMEM((2, 32), jnp.int32),
-            pltpu.VMEM((6, 512), jnp.int32),
             pltpu.VMEM((640, 80), f32),
             pltpu.VMEM((TILES, 5, 64, 128), f32),
             pltpu.VMEM((6, TILES, 80, 128), f32),
             pltpu.VMEM((8, 80, 128), f32),
             pltpu.VMEM((8, 80, 128), f32),
             pltpu.VMEM((6, TILES, 80, 128), f32),
-            pltpu.VMEM((6, TILES, 80, 128), f32),
             pltpu.VMEM((6, TILES, 16, 128), f32),
-            pltpu.VMEM((TILES, 5, 64, 128), f32),
             pltpu.VMEM((2, 5, 64, 128), f32),
             pltpu.VMEM((2, 80, 128), f32),
             pltpu.VMEM((2, 80, 128), f32),
             pltpu.VMEM((2, 24, 128), f32),
-            pltpu.VMEM((2, 24, 128), f32),
             pltpu.VMEM((8, 128), jnp.int32),
+            pltpu.VMEM((4, TILES, 80, 128), f32),
             pltpu.VMEM((TILES, 5, 64, 128), f32),
             pltpu.VMEM((TILES, 5, 64, 128), f32),
             pltpu.SemaphoreType.DMA((TILES,)),
@@ -620,7 +668,19 @@
             )
         )
     )
-    return step_size[0] * residual
+    return pl.pallas_call(
+        close_kernel,
+        out_shape=jax.ShapeDtypeStruct(state.shape, f32),
+        in_specs=[vmem] * 5 + [pl.BlockSpec(memory_space=pltpu.SMEM)],
+        out_specs=pl.BlockSpec(memory_space=pltpu.HBM),
+        scratch_shapes=[
+            pltpu.VMEM((TILES, 5, 64, 128), f32),
+            pltpu.VMEM((5, 64, 128), f32),
+            pltpu.SemaphoreType.DMA((TILES,)),
+        ],
+        compiler_params=pltpu.CompilerParams(vmem_limit_bytes=8 * 1024 * 1024),
+        name="close",
+    )(*(pltpu.with_memory_space_constraint(part, pltpu.VMEM) for part in parts), step_size)
 
 
 def solution(mesh):

time: 24.9 us -> 23.9 us (0.960)
  other arithmetic: 0.89 us -> 0 us
    mul x1 -> x0, other arithmetic: 0.89 us -> none  [body(): return step_size[0] * residual]
    pallas_call x1 -> x2, Pallas kernels: 23.2 us -> 23.2 us  [the longest x1 21.5 us: body(): pl.pallas_call(functools.partial(kernel, count), out_shape=kept, in_specs...]
where the time goes in v3:
time: 23.9 us; the launch traced here: 23.8 us
  Pallas kernels  23.2 us (97%)
  between operations  0.66 us (3%)
    pallas_call x1, Pallas kernels, body(): pl.pallas_call(functools.partial(kernel, count), out_shape=kept, in_specs...  21.5 us
    pallas_call x1, Pallas kernels, body(): pl.pallas_call(close_kernel, out_shape=jax.ShapeDtypeStruct(state.shape,...  1.71 us

profile of v3, /device:TPU:0, one launch (start us, length us, event | category | flops | bytes accessed | tf_op | source)
XLA Modules:
  0.0 23.8 jit_solution(16028778042935737600)
XLA Ops:
  0.7 21.5 %section.1 = (f32[4,5,64,128]{3,2,1,0:T(8,128)S(1)}, f32[6,4,80,128]{3,2,1,0:T(8,128)S(1)}, f32[2,24,128]{2,1,0:T(8,128)S(1)}, s32[6,512]{1,0:T(8,128)S(1)}, s32[1,512]{1,0:T(1,128)S(1)}) custom-call(f32[5,64,512]{2,1,0:T(8,128)} %state_hbm.1, s32[1,512]{1,0:T(1,128)} %bitcast.2, s32[8,128]{1,0:T(8,128)} %send_hbm.1, s32[6,512]{1,0:T(8,128)} %partner_hbm.1, ...), custom_call_target="tpu_custom_call" | custom-call | tf_op jit(solution)/shard_map/section/pallas_call | solution.py:618
  22.1 1.7 %close.1 = f32[5,64,512]{2,1,0:T(8,128)} custom-call(f32[4,5,64,128]{3,2,1,0:T(8,128)S(1)} %get-tuple-element.10.res, f32[6,4,80,128]{3,2,1,0:T(8,128)S(1)} %get-tuple-element.11.own, f32[2,24,128]{2,1,0:T(8,128)S(1)} %get-tuple-element.12.rrcv, s32[6,512]{1,0:T(8,128)S(1)} %get-tuple-element.13.source_ref, s32[1,512]{1,0:T(1,128)S(1)} %get-tuple-element.14.levels_ref, ...), custom_call_target="tpu_custom_call" | custom-call | tf_op jit(solution)/shard_map/close/pallas_call | solution.py:671

commit v4 on v3

--- a/solution.py
+++ b/solution.py
@@ -2,6 +2,7 @@
 
 import jax
 import jax.numpy as jnp
+import ml_dtypes
 import numpy as np
 from jax import lax
 from jax.experimental import pallas as pl
@@ -9,7 +10,6 @@
 from jax.sharding import PartitionSpec as P
 
 GAMMA = 1.4
-HIGHEST = lax.Precision.HIGHEST
 MESH = pl.DeviceIdType.MESH
 TILES = 4
 SIDE = (0, 0, 1, 1, 2, 2)
@@ -55,7 +55,17 @@
     five = np.eye(5)
     forth = [np.kron(five, np.kron(ahead[q % 2], ahead[q // 2])) for q in range(4)]
     home = [np.kron(five, np.kron(back[q % 2], back[q // 2])) for q in range(4)]
-    return np.concatenate(forth + home, axis=0).astype(np.float32)
+    whole = np.concatenate(forth + home, axis=0)
+    upper_part = whole.astype(ml_dtypes.bfloat16)
+    lower_part = (whole - upper_part.astype(np.float64)).astype(ml_dtypes.bfloat16)
+    return np.concatenate([upper_part, upper_part, lower_part], axis=1)
+
+
+def product(matrix, columns):
+    coarse = columns.astype(jnp.bfloat16)
+    rest = (columns - coarse.astype(jnp.float32)).astype(jnp.bfloat16)
+    stacked = jnp.concatenate([coarse, rest, coarse], axis=0)
+    return jnp.dot(matrix, stacked, preferred_element_type=jnp.float32)
 
 
 def lanes_of(tile, index):
@@ -295,13 +305,7 @@
     def send_step(c, carry):
         p = lax.rem(4 - c, 4)
         outgoing(p)
-        fluxes_of(c)
         outgoing(p + 4)
-        slopes_of(c)
-        own_fluxes_of(c)
-        for v in range(5):
-            lift_j[c, v] = jnp.zeros((64, 128), jnp.float32)
-            lift_k[c, v] = jnp.zeros((64, 128), jnp.float32)
         return carry
 
     small[0].wait()
@@ -352,6 +356,12 @@
     small[4].wait()
 
     def local_step(c, carry):
+        fluxes_of(c)
+        slopes_of(c)
+        own_fluxes_of(c)
+        for v in range(5):
+            lift_j[c, v] = jnp.zeros((64, 128), jnp.float32)
+            lift_k[c, v] = jnp.zeros((64, 128), jnp.float32)
         span = pl.ds(pl.multiple_of(128 * c, 128), 128)
         for f in range(6):
             tile, place = placed(partner_ref[f : f + 1, span])
@@ -387,9 +397,7 @@
             pltpu.roll(states[0], 80, axis=1),
         ),
     )
-    near = jnp.dot(
-        matrix_ref[0:320], big, precision=HIGHEST, preferred_element_type=jnp.float32
-    )
+    near = product(matrix_ref[0:320], big)
     nears = [
         jnp.where(lane80 < 80, near[0:80], near[80:160]),
         jnp.where(lane80 < 40, near[160:240], near[240:320]),
@@ -417,12 +425,8 @@
                 axis=0,
             )
         )
-    home_a = jnp.dot(
-        matrix_ref[320:480], stars[0], precision=HIGHEST, preferred_element_type=jnp.float32
-    )
-    home_b = jnp.dot(
-        matrix_ref[480:640], stars[1], precision=HIGHEST, preferred_element_type=jnp.float32
-    )
+    home_a = product(matrix_ref[320:480], stars[0])
+    home_b = product(matrix_ref[480:640], stars[1])
     together = (
         pltpu.roll(home_a[0:80], 88, axis=1)
         + pltpu.roll(home_a[80:160], 48, axis=1)
@@ -626,7 +630,7 @@
             pltpu.VMEM((5, 40), jnp.int32),
             pltpu.VMEM((1, 40), jnp.int32),
             pltpu.VMEM((2, 32), jnp.int32),
-            pltpu.VMEM((640, 80), f32),
+            pltpu.VMEM((640, 240), jnp.bfloat16),
             pltpu.VMEM((TILES, 5, 64, 128), f32),
             pltpu.VMEM((6, TILES, 80, 128), f32),
             pltpu.VMEM((8, 80, 128), f32),

time: 23.9 us -> 23.6 us (0.987)
  Pallas kernels: 23.2 us -> 22.8 us
    pallas_call x1, Pallas kernels: 21.5 us -> 21.1 us  [body(): pl.pallas_call(functools.partial(kernel, count), out_shape=kept, in_specs...]
where the time goes in v4:
time: 23.6 us; the launch traced here: 23.5 us
  Pallas kernels  22.8 us (97%)
  between operations  0.66 us (3%)
    pallas_call x1, Pallas kernels, body(): pl.pallas_call(functools.partial(kernel, count), out_shape=kept, in_specs...  21.1 us
    pallas_call x1, Pallas kernels, body(): pl.pallas_call(close_kernel, out_shape=jax.ShapeDtypeStruct(state.shape,...  1.71 us

profile of v4, /device:TPU:0, one launch (start us, length us, event | category | flops | bytes accessed | tf_op | source)
XLA Modules:
  0.0 23.5 jit_solution(8311408210315922299)
XLA Ops:
  0.7 21.1 %section.1 = (f32[4,5,64,128]{3,2,1,0:T(8,128)S(1)}, f32[6,4,80,128]{3,2,1,0:T(8,128)S(1)}, f32[2,24,128]{2,1,0:T(8,128)S(1)}, s32[6,512]{1,0:T(8,128)S(1)}, s32[1,512]{1,0:T(1,128)S(1)}) custom-call(f32[5,64,512]{2,1,0:T(8,128)} %state_hbm.1, s32[1,512]{1,0:T(1,128)} %bitcast.2, s32[8,128]{1,0:T(8,128)} %send_hbm.1, s32[6,512]{1,0:T(8,128)} %partner_hbm.1, ...), custom_call_target="tpu_custom_call" | custom-call | tf_op jit(solution)/shard_map/section/pallas_call | solution.py:622
  21.8 1.7 %close.1 = f32[5,64,512]{2,1,0:T(8,128)} custom-call(f32[4,5,64,128]{3,2,1,0:T(8,128)S(1)} %get-tuple-element.10.res, f32[6,4,80,128]{3,2,1,0:T(8,128)S(1)} %get-tuple-element.11.own, f32[2,24,128]{2,1,0:T(8,128)S(1)} %get-tuple-element.12.rrcv, s32[6,512]{1,0:T(8,128)S(1)} %get-tuple-element.13.source_ref, s32[1,512]{1,0:T(1,128)S(1)} %get-tuple-element.14.levels_ref, ...), custom_call_target="tpu_custom_call" | custom-call | tf_op jit(solution)/shard_map/close/pallas_call | solution.py:675

commit v5 on v4

--- a/solution.py
+++ b/solution.py
@@ -351,7 +351,7 @@
                 value = jnp.where(tile == f * TILES + c, lanes_of(tr[f, c], place), value)
         mor[m] = value
 
-    for p in (3, 7, 2, 6, 1, 5):
+    for p in (7, 3, 6, 2, 5, 1):
         trace_copy(p).start()
     small[4].wait()
 

time: 23.6 us -> 23.6 us (level)
  no operation moved by 1% of the time
where the time goes in v5:
time: 23.6 us; the launch traced here: 23.5 us
  Pallas kernels  22.8 us (97%)
  between operations  0.66 us (3%)
    pallas_call x1, Pallas kernels, body(): pl.pallas_call(functools.partial(kernel, count), out_shape=kept, in_specs...  21.1 us
    pallas_call x1, Pallas kernels, body(): pl.pallas_call(close_kernel, out_shape=jax.ShapeDtypeStruct(state.shape,...  1.71 us

profile of v5, /device:TPU:0, one launch (start us, length us, event | category | flops | bytes accessed | tf_op | source)
XLA Modules:
  0.0 23.5 jit_solution(17826235320399478976)
XLA Ops:
  0.7 21.1 %section.1 = (f32[4,5,64,128]{3,2,1,0:T(8,128)S(1)}, f32[6,4,80,128]{3,2,1,0:T(8,128)S(1)}, f32[2,24,128]{2,1,0:T(8,128)S(1)}, s32[6,512]{1,0:T(8,128)S(1)}, s32[1,512]{1,0:T(1,128)S(1)}) custom-call(f32[5,64,512]{2,1,0:T(8,128)} %state_hbm.1, s32[1,512]{1,0:T(1,128)} %bitcast.2, s32[8,128]{1,0:T(8,128)} %send_hbm.1, s32[6,512]{1,0:T(8,128)} %partner_hbm.1, ...), custom_call_target="tpu_custom_call" | custom-call | tf_op jit(solution)/shard_map/section/pallas_call | solution.py:622
  21.8 1.7 %close.1 = f32[5,64,512]{2,1,0:T(8,128)} custom-call(f32[4,5,64,128]{3,2,1,0:T(8,128)S(1)} %get-tuple-element.10.res, f32[6,4,80,128]{3,2,1,0:T(8,128)S(1)} %get-tuple-element.11.own, f32[2,24,128]{2,1,0:T(8,128)S(1)} %get-tuple-element.12.rrcv, s32[6,512]{1,0:T(8,128)S(1)} %get-tuple-element.13.source_ref, s32[1,512]{1,0:T(1,128)S(1)} %get-tuple-element.14.levels_ref, ...), custom_call_target="tpu_custom_call" | custom-call | tf_op jit(solution)/shard_map/close/pallas_call | solution.py:675
